TPU v7x, 768 devices: a whole 4x8x12 slice. The times are simulated.
768 devices in a mesh: feat: 96 (over z, y), batch: 8 (over x, core).
Axes of the slice: x: 4, y: 8, z: 12, core: 2. Of those that a mesh axis runs over, the one named last changes fastest.
Arguments:
- features: bfloat16 [1056, 65536], P('feat'), may hold values from -6 to 6
- nbr_ids: int32 [16896, 15], P('batch'), may hold values from 0 to 65535
- nbr_counts: int32 [16896], P('batch'), may hold values from 1 to 15
- self_ids: int32 [16896], P('batch'), may hold values from 0 to 65535
- seed_counts: int32 [1536], P('batch'), may hold values from 1 to 10
- labels: int32 [1536], P('batch'), may hold values from 0 to 171
- w1_self: bfloat16 [1056, 256], P('feat'), may hold values from -0.1875 to 0.1875
- w1_nbr: bfloat16 [1056, 256], P('feat'), may hold values from -0.1875 to 0.1875
- w2_self: bfloat16 [256, 256], replicated, may hold values from -0.375 to 0.375
- w2_nbr: bfloat16 [256, 256], replicated, may hold values from -0.375 to 0.375
- w3: bfloat16 [256, 172], replicated, may hold values from -0.375 to 0.375
Outputs:
- dw1_self: float32 [1056, 256], P('feat')
- dw1_nbr: float32 [1056, 256], P('feat')
- dw2_self: float32 [256, 256], replicated
- dw2_nbr: float32 [256, 256], replicated
- dw3: float32 [256, 172], replicated
Inputs may be any that keep to these rules, and one draw needn't show every extreme that they name: `nbr_ids`: ids beyond a target's count are padding and unused.
All inputs are finite; a program needn't handle non-finite values.
Results may differ from a plain program's by a relative error of at most 0.0059.
Values may be sent and summed in bfloat16 or wider, within the bound.
No kernel may reach another device: no remote copies, remote signals or barrier semaphores. Data moves between devices by JAX's collectives and lax.ppermute only.
A program may use at most 64 MiB of HBM per device.

v0:
```python
import jax
import jax.numpy as jnp
from jax import lax
from jax.sharding import PartitionSpec as P

SEED_DEV = 2


def inner_rows(left, right):
    return lax.dot_general(
        left, right, (((0,), (0,)), ((), ())), preferred_element_type=jnp.float32
    )


def outer_cols(left, right):
    return lax.dot_general(
        left, right, (((1,), (1,)), ((), ())), preferred_element_type=jnp.float32
    )


def smooth_act(value):
    return value * jax.nn.sigmoid(value)


def smooth_slope(value):
    sigma = jax.nn.sigmoid(value)
    return sigma * (1.0 + value * (1.0 - sigma))


def masked_mean(values, counts):
    width = values.shape[1]
    valid_mask = lax.broadcasted_iota(jnp.int32, (values.shape[0], width), 1) < counts[:, None]
    summed = jnp.sum(
        jnp.where(valid_mask[:, :, None], values.astype(jnp.float32), jnp.float32(0.0)), axis=1
    )
    return summed / counts[:, None].astype(jnp.float32)


def column_mean(picked, counts):
    fan_width = picked.shape[1]
    valid_mask = lax.broadcasted_iota(jnp.int32, (fan_width, counts.shape[0]), 0) < counts[None, :]
    summed = jnp.sum(
        jnp.where(valid_mask[None, :, :], picked.astype(jnp.float32), jnp.float32(0.0)), axis=1
    )
    return summed / counts[None, :].astype(jnp.float32)


def upper_step(act_one, counts, targets, w2_self, w2_nbr, w3, loss_scale):
    seeds = counts.shape[0]
    hidden = act_one.shape[1]
    groups = act_one.reshape(seeds, -1, hidden)
    head_rows = groups[:, 0]
    tail_rows = groups[:, 1:]
    fan_two = tail_rows.shape[1]
    mean_two = masked_mean(tail_rows, counts).astype(jnp.bfloat16)
    pre_two = jnp.dot(head_rows, w2_self, preferred_element_type=jnp.float32) + jnp.dot(
        mean_two, w2_nbr, preferred_element_type=jnp.float32
    )
    act_two = smooth_act(pre_two).astype(jnp.bfloat16)
    logits = jnp.dot(act_two, w3, preferred_element_type=jnp.float32)
    shifted = logits - jnp.max(logits, axis=1, keepdims=True)
    expsum = jnp.exp(shifted)
    probability = expsum / jnp.sum(expsum, axis=1, keepdims=True)
    onehot = (lax.broadcasted_iota(jnp.int32, logits.shape, 1) == targets[:, None]).astype(
        jnp.float32
    )
    grad_three = ((probability - onehot) * loss_scale).astype(jnp.bfloat16)
    grad_w3 = inner_rows(act_two, grad_three)
    grad_two = (outer_cols(grad_three, w3) * smooth_slope(pre_two)).astype(jnp.bfloat16)
    grad_w2s = inner_rows(head_rows, grad_two)
    grad_w2n = inner_rows(mean_two, grad_two)
    grad_head = outer_cols(grad_two, w2_self)
    grad_mean = outer_cols(grad_two, w2_nbr)
    kept_mask = lax.broadcasted_iota(jnp.int32, (seeds, fan_two), 1) < counts[:, None]
    grad_tail = jnp.where(
        kept_mask[:, :, None],
        grad_mean[:, None, :] / counts[:, None, None].astype(jnp.float32),
        jnp.float32(0.0),
    )
    grad_act = jnp.concatenate([grad_head[:, None, :], grad_tail], axis=1).reshape(-1, hidden)
    return (grad_w3, grad_w2s, grad_w2n, grad_act)


def owner_tail(pre_one, own_cols, aggregated, seed_counts, labels, w2_self, w2_nbr, w3, loss_scale):
    feat_index = lax.axis_index("feat")
    act_one = smooth_act(pre_one).astype(jnp.bfloat16)
    seed_mine = lax.dynamic_slice_in_dim(seed_counts, feat_index * SEED_DEV, SEED_DEV, 0)
    label_mine = lax.dynamic_slice_in_dim(labels, feat_index * SEED_DEV, SEED_DEV, 0)
    grad_w3, grad_w2s, grad_w2n, grad_act = upper_step(
        act_one, seed_mine, label_mine, w2_self, w2_nbr, w3, loss_scale
    )
    grad_w3, grad_w2s, grad_w2n = lax.psum((grad_w3, grad_w2s, grad_w2n), ("feat", "batch"))
    grad_one = (grad_act * smooth_slope(pre_one)).astype(jnp.bfloat16)
    grad_piece = lax.all_gather(grad_one, "feat", axis=0, tiled=True)
    grad_w1s = jnp.dot(own_cols, grad_piece, preferred_element_type=jnp.float32)
    grad_w1n = jnp.dot(aggregated, grad_piece, preferred_element_type=jnp.float32)
    grad_w1s, grad_w1n = lax.psum((grad_w1s, grad_w1n), "batch")
    return (grad_w1s, grad_w1n, grad_w2s, grad_w2n, grad_w3)


def local(
    features,
    nbr_ids,
    nbr_counts,
    self_ids,
    seed_counts,
    labels,
    w1_self,
    w1_nbr,
    w2_self,
    w2_nbr,
    w3,
):
    feat_size = lax.axis_size("feat")
    batch_size = lax.axis_size("batch")
    loss_scale = 1.0 / (SEED_DEV * feat_size * batch_size)
    picked = jnp.take(features, nbr_ids.T, axis=1)
    aggregated = column_mean(picked, nbr_counts).astype(jnp.bfloat16)
    own_cols = jnp.take(features, self_ids, axis=1)
    pre_one = lax.psum_scatter(
        inner_rows(own_cols, w1_self) + inner_rows(aggregated, w1_nbr),
        "feat",
        scatter_dimension=0,
        tiled=True,
    )
    results = owner_tail(
        pre_one, own_cols, aggregated, seed_counts, labels, w2_self, w2_nbr, w3, loss_scale
    )
    return results


def solution(mesh):
    in_specs = (
        P("feat", None),
        P("batch", None),
        P("batch"),
        P("batch"),
        P("batch"),
        P("batch"),
        P("feat", None),
        P("feat", None),
        P(),
        P(),
        P(),
    )
    out_specs = (P("feat", None), P("feat", None), P(), P(), P())
    return jax.shard_map(local, mesh=mesh, in_specs=in_specs, out_specs=out_specs, check_vma=False)
```

profile of v0, /device:TPU:1, one launch (start us, length us, event | category | flops | bytes accessed | tf_op | source)
XLA Modules:
  0.0 937.3 jit_solution(5623789034196856200)
XLA Ops:
  12.3 12.8 %copy.22 = bf16[11,65536]{0,1:T(8,128)(2,1)} copy(bf16[11,65536]{1,0:T(8,128)(2,1)} %param.11) | data formatting | bytes 2883584 | tf_op args[0]
  25.1 12.0 %gather_fusion = bf16[2112,11]{1,0:T(8,128)(2,1)S(1)} fusion(bf16[11,65536]{0,1:T(8,128)(2,1)} %copy.22, s32[3072]{0:T(1024)S(1)} %pad_clamp_fusion.1), kind=kCustom, calls=%fused_computation | custom fusion | bytes 101376 | tf_op jit(solution)/shard_map/jit(_take)/gather | solution.py:119
  37.1 113.8 %gather_fusion.1 = bf16[31680,11]{1,0:T(8,128)(2,1)} fusion(bf16[11,65536]{0,1:T(8,128)(2,1)} %copy.22, s32[31744]{0:T(1024)S(1)} %pad_clamp_fusion), kind=kCustom, calls=%fused_computation.1 | custom fusion | bytes 1520640 | tf_op jit(solution)/shard_map/jit(_take)/gather | solution.py:117
  150.9 13.9 %select_reduce_fusion = f32[2112,11]{1,0:T(8,128)S(1)} fusion(bf16[15,2112,11]{2,1,0:T(8,128)(2,1)} %bitcast.33, pred[15,2112]{1,0:T(8,128)(4,1)S(1)} %get-tuple-element.14, pred[15,2112]{1,0:T(8,128)(4,1)S(1)} %get-tuple-element.15), kind=kLoop, calls=%fused_computation.2 | loop fusion | flops 1370688 | bytes 853248 | tf_op jit(solution)/shard_map/reduce_sum | solution.py:42
  165.1 1.6 fusion.2
  167.2 192.5 %fusion = f32[24,256]{1,0:T(8,128)S(1)} fusion(f32[2112,256]{1,0:T(8,128)S(1)} %convolution_add_fusion), kind=kCustom, calls=%all-reduce-scatter | all-reduce-scatter fusion | flops 589825 | bytes 2191360
  359.8 1.3 collective-permute-start.6
  361.1 1.3 collective-permute-start.5
  362.4 1.3 collective-permute-start.4
  363.7 1.3 collective-permute-start.3
  365.0 4.6 collective-permute-start.7
  370.5 6.6 collective-permute-start.2
  377.2 2.2 collective-permute-start.1
  379.4 2.8 collective-permute-start
  382.4 1.3 dynamic-slice.4
  384.4 1.1 concatenate.4
  385.9 1.2 fusion.18
  392.5 159.4 %all-gather.3.cloned.1.call-done = bf16[96,22,256]{2,1,0:T(8,128)(2,1)} async-done(((bf16[1,22,256]{2,1,0:T(8,128)(2,1)}), bf16[96,22,256]{2,1,0:T(8,128)(2,1)}) %all-gather.3.cloned.1.call-update) | async-done | bytes 1081360 | tf_op jit(solution)/shard_map/all_gather | solution.py:94
  551.9 1.4 reshape.99
  554.2 29.0 %all-reduce.3 = (f32[11,256]{1,0:T(8,128)}, f32[11,256]{1,0:T(8,128)}) all-reduce(f32[11,256]{1,0:T(8,128)S(1)} %fusion.3, f32[11,256]{1,0:T(8,128)S(1)} %fusion.19), channel_id=1, replica_groups=mesh['feat'=96,'batch'=8] {'batch'}, use_global_device_ids=true, to_apply=%region_5.6 | all-reduce | flops 5632 | bytes 45056 | tf_op jit(solution)/shard_map/psum | solution.py:97
  583.2 341.7 %all-reduce.6.cloned.1.call-done = (f32[256,256]{1,0:T(8,128)}, f32[256,256]{1,0:T(8,128)}, f32[256,172]{0,1:T(8,128)}) async-done(((f32[256,256]{1,0:T(8,128)}, f32[256,256]{1,0:T(8,128)}, f32[256,172]{0,1:T(8,128)}), (f32[256,256]{1,0:T(8,128)}, f32[256,256]{1,0:T(8,128)}, f32[256,172]{0,1:T(8,128)})) %all-reduce.6.cloned.1.call-update) | async-done | bytes 700432 | tf_op jit(solution)/shard_map/psum | solution.py:92
  924.9 1.7 copy.37
  926.6 1.7 copy.38
  928.2 1.6 copy.39
  (58 shorter events, 12.8 us)
Async XLA Ops:
  8.0 377.8 %copy-start = (bf16[256,256]{1,0:T(8,128)(2,1)S(1)}, bf16[256,256]{1,0:T(8,128)(2,1)}, u32[]{:S(2)}) copy-start(bf16[256,256]{1,0:T(8,128)(2,1)} %param.20) | copy-start | bytes 393220
  8.0 543.9 %all-gather.3.cloned.1.call-start = ((), (), s32[]{:S(2)}) async-start(), calls=%async_computation | async-start | bytes 1191936 | tf_op jit(solution)/shard_map/all_gather | solution.py:94
  150.9 14.3 %copy-start.2 = (bf16[11,256]{1,0:T(8,128)(2,1)S(1)}, bf16[11,256]{1,0:T(8,128)(2,1)}, u32[]{:S(2)}) copy-start(bf16[11,256]{1,0:T(8,128)(2,1)} %param.17) | copy-start | bytes 16900
  164.8 2.0 copy-start.3
  167.2 202.4 %copy-start.4 = (s32[192]{0:T(256)S(1)}, s32[192]{0:T(256)}, u32[]{:S(2)}) copy-start(s32[192]{0:T(256)} %param.15) | copy-start | bytes 2308
  167.2 215.1 %copy-start.5 = (s32[192]{0:T(256)S(1)}, s32[192]{0:T(256)}, u32[]{:S(2)}) copy-start(s32[192]{0:T(256)} %param.16) | copy-start | bytes 2308
  167.2 218.4 %copy-start.1 = (bf16[256,256]{1,0:T(8,128)(2,1)S(1)}, bf16[256,256]{1,0:T(8,128)(2,1)}, u32[]{:S(2)}) copy-start(bf16[256,256]{1,0:T(8,128)(2,1)} %param.19) | copy-start | bytes 393220
  359.8 17.4 %collective-permute-start.6 = (f32[24,256]{1,0:T(8,128)S(1)}, f32[24,256]{1,0:T(8,128)S(1)}, u32[]{:S(2)}, u32[]{:S(2)}) collective-permute-start(f32[24,256]{1,0:T(8,128)S(1)} %fusion), channel_id=1, source_target_pairs={{0,56},{8,64},{16,72},{24,80},{32,88},{40,96},{48,104},{56,112},{6... | collective-permute-start | bytes 73736
  361.1 18.3 %collective-permute-start.5 = (f32[24,256]{1,0:T(8,128)S(1)}, f32[24,256]{1,0:T(8,128)S(1)}, u32[]{:S(2)}, u32[]{:S(2)}) collective-permute-start(f32[24,256]{1,0:T(8,128)S(1)} %fusion), channel_id=1, source_target_pairs={{0,48},{8,56},{16,64},{24,72},{32,80},{40,88},{48,96},{56,104},{64... | collective-permute-start | bytes 73736
  362.4 21.9 %collective-permute-start.4 = (f32[24,256]{1,0:T(8,128)S(1)}, f32[24,256]{1,0:T(8,128)S(1)}, u32[]{:S(2)}, u32[]{:S(2)}) collective-permute-start(f32[24,256]{1,0:T(8,128)S(1)} %fusion), channel_id=1, source_target_pairs={{0,40},{8,48},{16,56},{24,64},{32,72},{40,80},{48,88},{56,96},{64,... | collective-permute-start | bytes 73736
  363.7 20.7 %collective-permute-start.3 = (f32[24,256]{1,0:T(8,128)S(1)}, f32[24,256]{1,0:T(8,128)S(1)}, u32[]{:S(2)}, u32[]{:S(2)}) collective-permute-start(f32[24,256]{1,0:T(8,128)S(1)} %fusion), channel_id=1, source_target_pairs={{0,32},{8,40},{16,48},{24,56},{32,64},{40,72},{48,80},{56,88},{64,... | collective-permute-start | bytes 73736
  365.0 5.5 collective-permute-start.7
  370.5 13.8 %collective-permute-start.2 = (f32[24,256]{1,0:T(8,128)S(1)}, f32[24,256]{1,0:T(8,128)S(1)}, u32[]{:S(2)}, u32[]{:S(2)}) collective-permute-start(f32[24,256]{1,0:T(8,128)S(1)} %fusion), channel_id=1, source_target_pairs={{0,24},{8,32},{16,40},{24,48},{32,56},{40,64},{48,72},{56,80},{64,... | collective-permute-start | bytes 73736
  377.2 7.2 collective-permute-start.1
  379.4 4.9 collective-permute-start
  389.5 535.4 %all-reduce.6.cloned.1.call-start = ((), (), s32[]{:S(2)}) async-start(), calls=%async_computation.1 | async-start | bytes 1409024 | tf_op jit(solution)/shard_map/psum | solution.py:92
Sparse Core Ops, SparseCore 0:
  389.7 162.1 all-gather.2
Sparse Core Ops, SparseCore 1:
  396.6 528.2 all-reduce.5
where the time goes:
time: 940 us; the launch traced here: 937 us
  waiting for transfers between devices  502 us (53%)
  blocking collectives  222 us (24%)
  local copies, waits for them, and re-layouts  148 us (16%)
  starting transfers between devices  21.5 us (2%)
  other arithmetic  19.5 us (2%)
  between operations  16.5 us (2%)
    psum x1, waiting for transfers between devices, owner_tail(): lax.psum((grad_w3, grad_w2s, grad_w2n), ('feat', 'batch'))  342 us
    unnamed x1, blocking collectives  193 us
    all_gather x1, waiting for transfers between devices, owner_tail(): grad_piece = lax.all_gather(grad_one, 'feat', axis=0, tiled=True)  159 us
    gather x1, local copies, waits for them, and re-layouts, local(): picked = jnp.take(features, nbr_ids.T, axis=1)  114 us
    psum x1, blocking collectives, owner_tail(): grad_w1s, grad_w1n = lax.psum((grad_w1s, grad_w1n), 'batch')  29 us
    unnamed x20, local copies, waits for them, and re-layouts  21.5 us
    unnamed x8, starting transfers between devices  21.4 us
  transfers between devices with their start and end apart: 10, of which 3 were waited for; matrix products, arithmetic and copies ran while one was open for 1% of the time, Pallas kernels for 0%

commit v1 on v0

v1 whole, which is shorter than its diff:
```python
import jax
import jax.numpy as jnp
from jax import lax
from jax.experimental import pallas as pl
from jax.experimental.pallas import tpu as pltpu
from jax.sharding import Mesh, PartitionSpec as P

NODES = 65536
COLS = 11
H = 256
C = 172
FAN1 = 15
FAN2 = 10
KEEP = 1 + FAN2
IDS = 1 + FAN1
SEEDS_B = 192
ROWS_B = SEEDS_B * KEEP
Z, Y, X, CORE = 12, 8, 4, 2
FEAT = Z * Y
BATCH = X * CORE
LOSS_SCALE = 1.0 / (SEEDS_B * BATCH)
OWN = 24
OWNERS = ROWS_B // OWN
GROUPS = 3
SLOTS = 8
SLOT_ROWS = NODES // SLOTS
WIDE = 24
PART = 104
BF16 = jnp.bfloat16
F32 = jnp.float32


def vmem():
    return pl.BlockSpec(memory_space=pltpu.VMEM)


def gather_kernel(ids_ref, x_ref, o_ref, table, own_ref, agg_ref):
    lane = lax.broadcasted_iota(jnp.int32, (1, 128), 1)

    @pl.loop(0, SLOT_ROWS // 128)
    def _(block):
        stacked = []
        for slot in range(SLOTS):
            start = pl.multiple_of(slot * SLOT_ROWS + block * 128, 128)
            stacked += [x_ref[:, pl.ds(start, 128)].astype(F32), jnp.ones((1, 128), F32), jnp.zeros((4, 128), F32)]
        turned = jnp.concatenate(stacked, 0).T
        for slot in range(SLOTS):
            start = pl.multiple_of(slot * SLOT_ROWS + block * 128, 128)
            table[pl.ds(start, 128), :] = jnp.where(lane // 16 == slot, turned, 0.0)

    table[pl.ds(NODES, 8), :] = jnp.zeros((8, 128), F32)

    @pl.loop(0, OWNERS)
    def _(owner):
        base = owner * (OWN * IDS)
        for i in range(OWN):
            group, row = i // 8, i % 8
            place = pl.ds(group * (OWNERS * 8) + owner * 8 + row, 1)
            picked = [table[pl.ds(ids_ref[base + i * IDS + j], 1), :] for j in range(IDS)]
            own_ref[place, :] = picked[0]
            terms = picked[1:]
            while len(terms) > 1:
                terms = [sum(terms[a : a + 2]) for a in range(0, len(terms), 2)]
            agg_ref[place, :] = terms[0]

    def fold(rows):
        for shift in (64, 32, 16):
            rows = rows + pltpu.roll(rows, shift, 1)
        return rows

    step = 64

    @pl.loop(0, OWNERS * 8 // step)
    def _(block):
        packed = jnp.zeros((step, 128), F32)
        for group in range(GROUPS):
            place = pl.ds(pl.multiple_of(group * (OWNERS * 8) + block * step, 8), step)
            own = fold(own_ref[place, :])
            agg = fold(agg_ref[place, :])
            mean = agg / agg[:, COLS : COLS + 1]
            both = jnp.where(lane % 32 < COLS, own, pltpu.roll(mean, COLS, 1))
            packed = jnp.where(lane // 32 == group, both, packed)
        packed = jnp.where(lane % 32 < 2 * COLS, packed, 0.0)
        o_ref[pl.ds(pl.multiple_of(block * step, step), step), :] = packed.astype(BF16)

    o_ref[pl.ds(OWNERS * 8, (FEAT - OWNERS) * 8), :] = jnp.zeros(((FEAT - OWNERS) * 8, 128), BF16)


def gather(ids, features):
    return pl.pallas_call(
        gather_kernel,
        out_shape=jax.ShapeDtypeStruct((FEAT * 8, 128), BF16),
        in_specs=[pl.BlockSpec(memory_space=pltpu.SMEM), vmem()],
        out_specs=vmem(),
        scratch_shapes=[
            pltpu.VMEM((NODES + 8, 128), F32),
            pltpu.VMEM((ROWS_B, 128), F32),
            pltpu.VMEM((ROWS_B, 128), F32),
        ],
        compiler_params=pltpu.CompilerParams(vmem_limit_bytes=50 * 1024 * 1024),
        cost_estimate=pl.CostEstimate(flops=80_000_000, bytes_accessed=150_000_000, transcendentals=0),
        name="gather",
    )(ids, features)


def project_kernel(r_ref, w_ref, o_ref):
    lane = lax.broadcasted_iota(jnp.int32, (1, 128), 1)
    total = jnp.zeros((OWN, H), F32)
    for quad in range(FEAT // 4):
        rows = r_ref[pl.ds(quad * 32, 32), :].astype(F32)
        left = []
        for group in range(GROUPS):
            mixed = jnp.zeros((8, 128), F32)
            for j in range(4):
                one = rows[j * 8 : (j + 1) * 8]
                shift = (j * WIDE - group * 32) % 128
                one = pltpu.roll(one, shift, 1) if shift else one
                mixed = jnp.where(lane // WIDE == j, one, mixed)
            left.append(mixed)
        left = jnp.concatenate(left, 0)[:, : 4 * WIDE].astype(BF16)
        right = w_ref[pl.ds(quad * 4 * WIDE, 4 * WIDE), :]
        total = total + jnp.dot(left, right, preferred_element_type=F32)
    o_ref[...] = total.astype(BF16)


def project(received, w1_all):
    return pl.pallas_call(
        project_kernel,
        out_shape=jax.ShapeDtypeStruct((OWN, H), BF16),
        in_specs=[vmem(), vmem()],
        out_specs=vmem(),
        compiler_params=pltpu.CompilerParams(vmem_limit_bytes=32 * 1024 * 1024),
        name="project",
    )(received, w1_all)


def sigmoid(value):
    return 1.0 / (1.0 + jnp.exp(-value))


def outer_cols(left, right):
    return lax.dot_general(left, right, (((1,), (1,)), ((), ())), preferred_element_type=F32)


def inner_rows(left, right):
    return lax.dot_general(left, right, (((0,), (0,)), ((), ())), preferred_element_type=F32)


def upper_kernel(z_ref, packed_ref, counts_ref, labels_ref, w2s_ref, w2n_ref, w3_ref, o_ref, g_ref):
    counts = counts_ref[...]
    scale = counts.astype(F32)
    head = None
    total = jnp.zeros((SEEDS_B, H), F32)
    for k in range(KEEP):
        value = z_ref[pl.ds(k * SEEDS_B, SEEDS_B), :].astype(F32)
        act = (value * sigmoid(value)).astype(BF16)
        if k == 0:
            head = act
        else:
            total = total + jnp.where(counts >= k, act.astype(F32), 0.0)
    mean_two = (total / scale).astype(BF16)
    pre_two = jnp.dot(head, w2s_ref[...], preferred_element_type=F32) + jnp.dot(
        mean_two, w2n_ref[...], preferred_element_type=F32
    )
    sig_two = sigmoid(pre_two)
    act_two = (pre_two * sig_two).astype(BF16)
    slope_two = sig_two * (1.0 + pre_two * (1.0 - sig_two))
    logits = jnp.dot(act_two, w3_ref[...], preferred_element_type=F32)
    expsum = jnp.exp(logits - jnp.max(logits, axis=1, keepdims=True))
    probability = expsum / jnp.sum(expsum, axis=1, keepdims=True)
    onehot = (lax.broadcasted_iota(jnp.int32, logits.shape, 1) == labels_ref[...]).astype(F32)
    grad_three = ((probability - onehot) * LOSS_SCALE).astype(BF16)
    grad_two = (outer_cols(grad_three, w3_ref[...]) * slope_two).astype(BF16)
    o_ref[pl.ds(0, H), :] = inner_rows(head, grad_two).astype(BF16)
    o_ref[pl.ds(H, H), :] = inner_rows(mean_two, grad_two).astype(BF16)
    o_ref[pl.ds(2 * H, H), :] = jnp.zeros((H, H), BF16)
    o_ref[pl.ds(2 * H, H), :C] = inner_rows(act_two, grad_three).astype(BF16)
    grad_head = outer_cols(grad_two, w2s_ref[...])
    grad_mean = outer_cols(grad_two, w2n_ref[...]) / scale
    for k in range(KEEP):
        value = z_ref[pl.ds(k * SEEDS_B, SEEDS_B), :].astype(F32)
        sig = sigmoid(value)
        slope = sig * (1.0 + value * (1.0 - sig))
        grad = grad_head if k == 0 else jnp.where(counts >= k, grad_mean, 0.0)
        grad = grad * slope
        for group in range(GROUPS):
            part = [grad[(GROUPS * a + group) * 8 :][:8] for a in range(8)]
            g_ref[group, pl.ds(k * 64, 64), :] = jnp.concatenate(part, 0).astype(BF16)
    turned = packed_ref[pl.ds(0, OWNERS * 8), :].astype(F32).T.astype(BF16)
    grad_one = jnp.zeros((32, H), F32)
    for group in range(GROUPS):
        left = turned[group * 32 : (group + 1) * 32]
        grad_one = grad_one + jnp.dot(left, g_ref[group], preferred_element_type=F32)
    o_ref[pl.ds(3 * H, 32), :] = grad_one.astype(BF16)
    rest = BATCH * PART - 3 * H - 32
    o_ref[pl.ds(3 * H + 32, rest), :] = jnp.zeros((rest, H), BF16)


def upper(pre_one, packed, counts, labels, w2_self, w2_nbr, w3):
    return pl.pallas_call(
        upper_kernel,
        out_shape=jax.ShapeDtypeStruct((BATCH * PART, H), BF16),
        in_specs=[vmem()] * 7,
        out_specs=vmem(),
        scratch_shapes=[pltpu.VMEM((GROUPS, OWNERS * 8, H), BF16)],
        compiler_params=pltpu.CompilerParams(vmem_limit_bytes=32 * 1024 * 1024),
        name="upper",
    )(pre_one, packed, counts, labels, w2_self, w2_nbr, w3)


def local(features, nbr_ids, nbr_counts, self_ids, seed_counts, labels, w1_self, w1_nbr, w2_self, w2_nbr, w3):
    w1_mine = jnp.concatenate([w1_self, w1_nbr, jnp.zeros((WIDE - 2 * COLS, H), BF16)], 0)
    w1_block = lax.all_to_all(jnp.broadcast_to(w1_mine[None], (Y, WIDE, H)), "y", 0, 0)
    w1_all = lax.all_gather(w1_block.reshape(Y * WIDE, H), "z", axis=0, tiled=True)

    valid = lax.broadcasted_iota(jnp.int32, (ROWS_B, FAN1), 1) < nbr_counts[:, None]
    ids = jnp.concatenate([self_ids[:, None], jnp.where(valid, nbr_ids, NODES)], 1)
    ids = ids.reshape(SEEDS_B, KEEP, IDS).transpose(1, 0, 2).reshape(-1)
    packed = gather(ids, features)

    received = lax.all_to_all(packed.reshape(FEAT, 8, 128), ("z", "y"), 0, 0)
    pre_mine = project(received.reshape(FEAT * 8, 128), w1_all)
    pre_one = lax.all_to_all(jnp.broadcast_to(pre_mine[None], (FEAT, OWN, H)), ("z", "y"), 0, 0)
    grads = upper(
        pre_one.reshape(FEAT * OWN, H), packed, seed_counts[:, None], labels[:, None], w2_self, w2_nbr, w3
    )
    shares = lax.all_to_all(grads.reshape(BATCH, PART, H), ("x", "core"), 0, 0)
    summed = jnp.sum(shares.astype(F32), axis=0)
    whole = lax.all_gather(summed, ("x", "core"), axis=0, tiled=True)
    first = 3 * H
    return (
        whole[first : first + COLS],
        whole[first + COLS : first + 2 * COLS],
        whole[:H],
        whole[H : 2 * H],
        whole[2 * H : 3 * H, :C],
    )


def solution(mesh):
    split = Mesh(mesh.devices.reshape(Z, Y, X, CORE), ("z", "y", "x", "core"))
    feat, batch = P(("z", "y"), None), P(("x", "core"))
    in_specs = (feat, P(("x", "core"), None), batch, batch, batch, batch, feat, feat, P(), P(), P())
    out_specs = (feat, feat, P(), P(), P())
    return jax.shard_map(local, mesh=split, in_specs=in_specs, out_specs=out_specs, check_vma=False)
```

time: 940 us -> 198 us (0.21)
  waiting for transfers between devices: 502 us -> 41 us
  blocking collectives: 222 us -> 80.5 us
  local copies, waits for them, and re-layouts: 148 us -> 9.09 us
  Pallas kernels: 0 us -> 44.4 us
  other arithmetic: 19.5 us -> 1.81 us
  starting transfers between devices: 21.5 us -> 6.15 us
    psum x1 -> x0, waiting for transfers between devices: 342 us -> none  [owner_tail(): lax.psum((grad_w3, grad_w2s, grad_w2n), ('feat', 'batch'))]
    unnamed x1 -> x0, blocking collectives: 193 us -> none
    all_gather x1, waiting for transfers between devices: 159 us -> 0.01 us  [local(): lax.all_gather(w1_block.reshape(Y * WIDE, H), 'z', axis=0, tiled=True)]
    gather x2 -> x0, local copies, waits for them, and re-layouts: 126 us -> none  [the longest x1 114 us: local(): picked = jnp.take(features, nbr_ids.T, axis=1)]
    all_to_all x0 -> x3, blocking collectives: none -> 66.2 us  [the longest x1 31.3 us: local(): received = lax.all_to_all(packed.reshape(FEAT, 8, 128), ('z', 'y'), 0, 0)]
    pallas_call x0 -> x3, Pallas kernels: none -> 44.4 us  [the longest x1 41.3 us: gather(): pl.pallas_call(gather_kernel, out_shape=jax.ShapeDtypeStruct((FEAT * 8, 1...]
    all_to_all x0 -> x1, waiting for transfers between devices: none -> 41 us  [local(): lax.all_to_all(jnp.broadcast_to(pre_mine[None], (FEAT, OWN, H)), ('z', 'y...]
    psum x1 -> x0, blocking collectives: 29 us -> none  [owner_tail(): grad_w1s, grad_w1n = lax.psum((grad_w1s, grad_w1n), 'batch')]
  transfers between devices with their start and end apart: 10 -> 2, of which waited for: 3 -> 1; matrix products, arithmetic and copies ran while one was open for 1% -> 2% of each run, Pallas kernels for 0% -> 21%
where the time goes in v1:
time: 198 us; the launch traced here: 197 us
  blocking collectives  80.5 us (41%)
  Pallas kernels  44.4 us (22%)
  waiting for transfers between devices  41 us (21%)
  between operations  14.2 us (7%)
  local copies, waits for them, and re-layouts  9.09 us (5%)
  starting transfers between devices  6.15 us (3%)
    pallas_call x1, Pallas kernels, gather(): pl.pallas_call(gather_kernel, out_shape=jax.ShapeDtypeStruct((FEAT * 8, 1...  41.3 us
    all_to_all x1, waiting for transfers between devices, local(): lax.all_to_all(jnp.broadcast_to(pre_mine[None], (FEAT, OWN, H)), ('z', 'y...  41 us
    all_to_all x1, blocking collectives, local(): received = lax.all_to_all(packed.reshape(FEAT, 8, 128), ('z', 'y'), 0, 0)  31.3 us
    all_to_all x1, blocking collectives, local(): shares = lax.all_to_all(grads.reshape(BATCH, PART, H), ('x', 'core'), 0, 0)  19.7 us
    all_to_all x1, blocking collectives, local(): lax.all_to_all(jnp.broadcast_to(w1_mine[None], (Y, WIDE, H)), 'y', 0, 0)  15.1 us
    all_gather x1, blocking collectives, local(): whole = lax.all_gather(summed, ('x', 'core'), axis=0, tiled=True)  14.3 us
    all_to_all x1, starting transfers between devices, local(): lax.all_to_all(jnp.broadcast_to(pre_mine[None], (FEAT, OWN, H)), ('z', 'y...  6.11 us
  transfers between devices with their start and end apart: 2, of which 1 were waited for; matrix products, arithmetic and copies ran while one was open for 2% of the time, Pallas kernels for 21%

profile of v1, /device:TPU:1, one launch (start us, length us, event | category | flops | bytes accessed | tf_op | source)
XLA Modules:
  0.0 197.1 jit_solution(1557318668094092236)
XLA Ops:
  7.3 0.8 maximum_maximum_fusion
  8.1 15.1 %all_to_all.20 = bf16[8,24,256]{2,1,0:T(8,128)(2,1)} all-to-all(bf16[8,24,256]{2,1,0:T(8,128)(2,1)S(1)} %broadcast_in_dim.29), channel_id=1, replica_groups=mesh['z'=12,'y'=8,'x'=4,'core'=2] {'y'}, dimensions={0} | all-to-all | bytes 196608 | tf_op jit(solution)/shard_map/all_to_all | solution.py:213
  23.3 0.9 fusion
  24.2 1.5 concatenate.12
  25.7 0.6 copy.30
  26.4 0.2 concatenate.11
  26.7 0.4 copy.31
  27.1 0.3 reshape.35.ids_ref
  27.4 0.9 copy-done
  28.3 41.3 %gather.1.packed_ref = bf16[768,128]{1,0:T(8,128)(2,1)S(1)} custom-call(s32[33792]{0:T(1024)S(1)} %reshape.35.ids_ref, bf16[11,65536]{1,0:T(8,128)(2,1)S(1)} %copy-done), custom_call_target="tpu_custom_call" | custom-call | flops 80000000 | bytes 150000000 | tf_op jit(solution)/shard_map/gather/pallas_call | solution.py:90
  69.6 31.3 %all_to_all.21 = bf16[96,8,128]{2,1,0:T(8,128)(2,1)S(1)} all-to-all(bf16[96,8,128]{2,1,0:T(8,128)(2,1)S(1)} %bitcast.12), channel_id=1, replica_groups=mesh['z'=12,'y'=8,'x'=4,'core'=2] {'z','y'}, dimensions={0} | all-to-all | bytes 393216 | tf_op jit(solution)/shard_map/all_to_all | solution.py:221
  100.9 1.3 copy-done.1
  102.2 0.4 project.1
  102.5 1.1 broadcast_in_dim.30
  103.7 6.1 %all-to-all-start.2 = ((bf16[96,24,256]{2,1,0:T(8,128)(2,1)}), bf16[96,24,256]{2,1,0:T(8,128)(2,1)S(1)}, u32[]{:S(2)}, u32[]{:S(2)}) async-start(bf16[96,24,256]{2,1,0:T(8,128)(2,1)} %broadcast_in_dim.30), calls=%async_computation.2 | async-start | bytes 2359296 | tf_op jit(solution)/shard_map/all_to_all | solution.py:223
  109.9 0.1 copy.32.counts_ref
  110.0 0.1 copy.33.labels_ref
  110.2 41.0 %all-to-all-done.2 = bf16[96,24,256]{2,1,0:T(8,128)(2,1)S(1)} async-done(((bf16[96,24,256]{2,1,0:T(8,128)(2,1)}), bf16[96,24,256]{2,1,0:T(8,128)(2,1)S(1)}, u32[]{:S(2)}, u32[]{:S(2)}) %all-to-all-start.2) | async-done | bytes 1179680 | tf_op jit(solution)/shard_map/all_to_all | solution.py:223
  151.1 2.8 %upper.1 = bf16[832,256]{1,0:T(8,128)(2,1)S(1)} custom-call(bf16[2304,256]{1,0:T(8,128)(2,1)S(1)} %bitcast.11, bf16[768,128]{1,0:T(8,128)(2,1)S(1)} %gather.1.packed_ref, s32[192,1]{1,0:T(8,128)S(1)} %copy.32.counts_ref, s32[192,1]{1,0:T(8,128)S(1)} %copy.33.labels_ref, bf16[256,256]{1,0:T(8,128)(2,1)S(1)} %copy-done.2, bf16[256,256]{1,0:T(8,128)(2,1)S(1)} %copy-done.3, ...), custom_call_target="tpu_custom_call" | custom-call | tf_op jit(solution)/shard_map/upper/pallas_call | solution.py:200
  153.9 19.7 %all_to_all.22 = bf16[8,104,256]{2,1,0:T(8,128)(2,1)S(1)} all-to-all(bf16[8,104,256]{2,1,0:T(8,128)(2,1)S(1)} %bitcast.13), channel_id=1, replica_groups=mesh['z'=12,'y'=8,'x'=4,'core'=2] {'x','core'}, dimensions={0} | all-to-all | bytes 851968 | tf_op jit(solution)/shard_map/all_to_all | solution.py:227
  173.7 14.3 %all_gather.7 = f32[832,256]{1,0:T(8,128)S(1)} all-gather(f32[104,256]{1,0:T(8,128)S(1)} %convert_reduce_fusion), channel_id=1, replica_groups=mesh['z'=12,'y'=8,'x'=4,'core'=2] {'x','core'}, dimensions={0}, use_global_device_ids=true | all-gather | bytes 958464 | tf_op jit(solution)/shard_map/all_gather | solution.py:229
  188.0 0.8 fusion.1
  188.8 0.6 fusion.2
  189.5 0.8 copy.35
  (25 shorter events, 0.5 us)
Async XLA Ops:
  7.2 93.7 %all-gather.2.cloned.1.call-start = ((), (), s32[]{:S(2)}) async-start(), calls=%async_computation.4 | async-start | bytes 1277952 | tf_op jit(solution)/shard_map/all_gather | solution.py:214
  25.7 0.7 copy-start.5
  26.7 1.6 copy-start
  100.9 1.3 copy-start.1
  103.6 6.1 %copy-start.4 = (bf16[256,172]{0,1:T(8,128)(2,1)S(1)}, bf16[256,172]{0,1:T(8,128)(2,1)}, u32[]{:S(2)}) copy-start(bf16[256,172]{0,1:T(8,128)(2,1)} %param.21) | copy-start | bytes 264196
  103.6 6.3 %copy-start.6 = (s32[192]{0:T(256)S(1)}, s32[192]{0:T(256)}, u32[]{:S(2)}) copy-start(s32[192]{0:T(256)} %param.15) | copy-start | bytes 2308
  103.6 6.4 %copy-start.7 = (s32[192]{0:T(256)S(1)}, s32[192]{0:T(256)}, u32[]{:S(2)}) copy-start(s32[192]{0:T(256)} %param.16) | copy-start | bytes 2308
  103.6 47.5 %copy-start.2 = (bf16[256,256]{1,0:T(8,128)(2,1)S(1)}, bf16[256,256]{1,0:T(8,128)(2,1)}, u32[]{:S(2)}) copy-start(bf16[256,256]{1,0:T(8,128)(2,1)} %w2s_ref.1) | copy-start | bytes 393220
  103.7 47.5 %copy-start.3 = (bf16[256,256]{1,0:T(8,128)(2,1)S(1)}, bf16[256,256]{1,0:T(8,128)(2,1)}, u32[]{:S(2)}) copy-start(bf16[256,256]{1,0:T(8,128)(2,1)} %w2n_ref.1) | copy-start | bytes 393220
  103.7 47.5 %all-to-all-start.2 = ((bf16[96,24,256]{2,1,0:T(8,128)(2,1)}), bf16[96,24,256]{2,1,0:T(8,128)(2,1)S(1)}, u32[]{:S(2)}, u32[]{:S(2)}) async-start(bf16[96,24,256]{2,1,0:T(8,128)(2,1)} %broadcast_in_dim.30), calls=%async_computation.2 | async-start | bytes 2359296 | tf_op jit(solution)/shard_map/all_to_all | solution.py:223
Sparse Core Ops, SparseCore 0:
  23.4 56.0 all-gather.1

commit v2 on v1

v2 whole, which is shorter than its diff:
```python
import jax
import jax.numpy as jnp
from jax import lax
from jax.experimental import pallas as pl
from jax.experimental.pallas import tpu as pltpu
from jax.sharding import Mesh, PartitionSpec as P

NODES = 65536
COLS = 11
H = 256
C = 172
FAN1 = 15
FAN2 = 10
IDS = 1 + FAN1
KEEP = 1 + FAN2
SEEDS_B = 192
ROWS_B = SEEDS_B * KEEP
Z, Y, X, CORE = 12, 8, 4, 2
BATCH = X * CORE
LOSS_SCALE = 1.0 / (SEEDS_B * BATCH)
SEEDS_Y = SEEDS_B // Y
ROWS_Y = SEEDS_Y * KEEP
GROUPS = 3
PACKED = ROWS_Y // GROUPS
SLOTS = 8
SLOT_ROWS = NODES // SLOTS
CHUNK = 128
LANES = -(-ROWS_B // CHUNK) * CHUNK
WIDE = 24
SEND = 144
SHARE = 24
ROWS_Z = Z * SHARE
BACK = 32 + 2 * SEEDS_Y
PART = 104
BF16 = jnp.bfloat16
F32 = jnp.float32
VMEM = pl.BlockSpec(memory_space=pltpu.VMEM)
SMEM = pl.BlockSpec(memory_space=pltpu.SMEM)


def gather_kernel(self_ref, nbr_ref, counts_ref, x_ref, w1s_ref, w1n_ref, o_ref, table, own_ref, agg_ref, stage, ids, near, sems):
    lane = lax.broadcasted_iota(jnp.int32, (1, 128), 1)

    def fetch(chunk, slot):
        at = chunk * CHUNK if isinstance(chunk, int) else pl.multiple_of(chunk * CHUNK, CHUNK)
        return pltpu.make_async_copy(ids.at[:, pl.ds(at, CHUNK)], near[slot], sems.at[slot])

    last = LANES - CHUNK
    ids[:, pl.ds(last, CHUNK)] = jnp.zeros((IDS, CHUNK), jnp.int32)
    valid = lax.broadcasted_iota(jnp.int32, (FAN1, ROWS_B), 0) < counts_ref[...]
    ids[pl.ds(0, FAN1), pl.ds(0, ROWS_B)] = jnp.where(valid, nbr_ref[...], NODES)
    ids[pl.ds(FAN1, 1), pl.ds(0, ROWS_B)] = self_ref[...]
    for slot in range(2):
        fetch(slot, slot).start()

    @pl.loop(0, SLOT_ROWS // 128, unroll=2)
    def _(block):
        stacked = []
        for slot in range(SLOTS):
            start = pl.multiple_of(slot * SLOT_ROWS + block * 128, 128)
            stacked += [x_ref[:, pl.ds(start, 128)].astype(F32), jnp.ones((1, 128), F32), jnp.zeros((4, 128), F32)]
        turned = jnp.concatenate(stacked, 0).T
        for slot in range(SLOTS):
            start = pl.multiple_of(slot * SLOT_ROWS + block * 128, 128)
            table[pl.ds(start, 128), :] = jnp.where(lane // 16 == slot, turned, 0.0)

    table[pl.ds(NODES, 8), :] = jnp.zeros((8, 128), F32)

    def take(chunk, slot, targets):
        first = chunk * CHUNK
        for i in range(targets):
            own_ref[pl.ds(first + i, 1), :] = table[pl.ds(near[slot][FAN1, i], 1), :]
            terms = [table[pl.ds(near[slot][j, i], 1), :] for j in range(FAN1)]
            while len(terms) > 1:
                terms = [sum(terms[a : a + 2]) for a in range(0, len(terms), 2)]
            agg_ref[pl.ds(first + i, 1), :] = terms[0]

    whole = ROWS_B // CHUNK

    @pl.loop(0, whole // 2)
    def _(pair):
        for slot in range(2):
            chunk = pair * 2 + slot
            fetch(chunk, slot).wait()
            take(chunk, slot, CHUNK)

            @pl.when(chunk + 2 <= whole)
            def _():
                fetch(chunk + 2, slot).start()

    fetch(whole, 0).wait()
    take(whole, 0, ROWS_B - whole * CHUNK)

    def halves(low, high, width):
        mask = lane % (2 * width) < width
        if high is None:
            return jnp.where(mask, low + pltpu.roll(low, 128 - width, 1), 0.0)
        moved = jnp.where(mask, pltpu.roll(low, 128 - width, 1), pltpu.roll(high, width, 1))
        return jnp.where(mask, low, high) + moved

    @pl.loop(0, Y)
    def _(block):
        for step in range(PACKED // 8):
            v = []
            for group in range(GROUPS):
                place = pl.ds(pl.multiple_of(block * ROWS_Y + group * PACKED + step * 8, 8), 8)
                v += [own_ref[place, :], agg_ref[place, :]]
            v = [halves(v[q], v[q + 4] if q < 2 else None, 64) for q in range(4)]
            v = [halves(v[q], v[q + 2], 32) for q in range(2)]
            stage[pl.ds(pl.multiple_of(block * SEND + step * 8, 8), 8), :] = halves(v[0], v[1], 16)

    w1 = jnp.concatenate([w1s_ref[...].astype(F32), w1n_ref[...].astype(F32), jnp.zeros((WIDE - 2 * COLS, H), F32)], 0)
    row = lax.broadcasted_iota(jnp.int32, (128, 128), 0)
    column = lax.broadcasted_iota(jnp.int32, (128, 128), 1)
    counter = jnp.where((row % 16 == COLS) & (row // 16 == column // 16), 1.0, 0.0).astype(BF16)

    @pl.loop(0, Y)
    def _(block):
        first = pl.multiple_of(block * SEND, 16)
        packed = stage[pl.ds(first, PACKED), :]
        counted = jnp.dot(packed.astype(BF16), counter, preferred_element_type=F32)
        packed = jnp.where((lane < GROUPS * 32) & (lane % 16 < COLS), packed / counted, 0.0)
        rest = jnp.zeros((SEND - PACKED - 2 * WIDE, 128), F32)
        message = jnp.concatenate([packed, w1[:, :128], w1[:, 128:], rest], 0)
        o_ref[pl.ds(first, SEND), :] = message.astype(BF16)


def gather(self_ids, nbr_ids, counts, features, w1_self, w1_nbr):
    return pl.pallas_call(
        gather_kernel,
        out_shape=jax.ShapeDtypeStruct((Y * SEND, 128), BF16),
        in_specs=[VMEM] * 6,
        out_specs=VMEM,
        scratch_shapes=[
            pltpu.VMEM((NODES + 8, 128), F32),
            pltpu.VMEM((ROWS_B, 128), F32),
            pltpu.VMEM((ROWS_B, 128), F32),
            pltpu.VMEM((Y * SEND, 128), F32),
            pltpu.VMEM((IDS, LANES), jnp.int32),
            [pltpu.SMEM((IDS, CHUNK), jnp.int32)] * 2,
            pltpu.SemaphoreType.DMA((2,)),
        ],
        compiler_params=pltpu.CompilerParams(vmem_limit_bytes=50 * 1024 * 1024),
        name="gather",
    )(self_ids, nbr_ids, counts, features, w1_self, w1_nbr)


def project_kernel(r_ref, o_ref, left_ref):
    lane = lax.broadcasted_iota(jnp.int32, (1, 128), 1)
    blocks = [r_ref[pl.ds(y * SEND, SEND), :].astype(F32) for y in range(Y)]
    right = []
    gap = jnp.zeros((16 - COLS, H), F32)
    for block in blocks:
        rows = jnp.concatenate([block[PACKED + half * WIDE :][:WIDE] for half in range(2)], 1)
        right += [rows[:COLS], gap, rows[COLS : 2 * COLS], gap]
    right = jnp.concatenate(right, 0).astype(BF16)
    left = []
    for group in range(GROUPS):
        halves = []
        for half in range(2):
            mixed = jnp.zeros((PACKED, 128), F32)
            for j in range(4):
                one = blocks[half * 4 + j][:PACKED]
                shift = (j - group) * 32 % 128
                one = pltpu.roll(one, shift, 1) if shift else one
                mixed = jnp.where(lane // 32 == j, one, mixed)
            halves.append(mixed)
        left.append(jnp.concatenate(halves, 1))
    left = jnp.concatenate(left, 0).astype(BF16)
    left_ref[...] = left
    total = jnp.dot(left, right, preferred_element_type=F32)
    o_ref[...] = jnp.concatenate([total, jnp.zeros((ROWS_Z - ROWS_Y, H), F32)], 0).astype(BF16)


def project(received):
    return pl.pallas_call(
        project_kernel,
        out_shape=(jax.ShapeDtypeStruct((ROWS_Z, H), BF16), jax.ShapeDtypeStruct((ROWS_Y, Y * 32), BF16)),
        in_specs=[VMEM],
        out_specs=(VMEM, VMEM),
        compiler_params=pltpu.CompilerParams(vmem_limit_bytes=32 * 1024 * 1024),
        name="project",
    )(received)


def spread_kernel(s_ref, o_ref):
    total = jnp.zeros((SHARE, H), F32)
    for pair in range(Z // 2):
        both = s_ref[pl.ds(pair * 2 * SHARE, 2 * SHARE), :].astype(F32)
        total = total + (both[:SHARE] + both[SHARE:])
    twice = jnp.concatenate([total, total], 0).astype(BF16)
    for pair in range(Z // 2):
        o_ref[pl.ds(pair * 2 * SHARE, 2 * SHARE), :] = twice


def spread(shares):
    return pl.pallas_call(
        spread_kernel,
        out_shape=jax.ShapeDtypeStruct((ROWS_Z, H), BF16),
        in_specs=[VMEM],
        out_specs=VMEM,
        name="spread",
    )(shares)


def sigmoid(value):
    return 1.0 / (1.0 + jnp.exp(-value))


def outer_cols(left, right):
    return lax.dot_general(left, right, (((1,), (1,)), ((), ())), preferred_element_type=F32)


def inner_rows(left, right):
    return lax.dot_general(left, right, (((0,), (0,)), ((), ())), preferred_element_type=F32)


def top(head, mean_two, labels, w2_self, w2_nbr, w3):
    pre_two = jnp.dot(head, w2_self, preferred_element_type=F32) + jnp.dot(mean_two, w2_nbr, preferred_element_type=F32)
    sig_two = sigmoid(pre_two)
    act_two = (pre_two * sig_two).astype(BF16)
    slope_two = sig_two * (1.0 + pre_two * (1.0 - sig_two))
    logits = jnp.dot(act_two, w3, preferred_element_type=F32)
    expsum = jnp.exp(logits - jnp.max(logits, axis=1, keepdims=True))
    probability = expsum / jnp.sum(expsum, axis=1, keepdims=True)
    onehot = (lax.broadcasted_iota(jnp.int32, logits.shape, 1) == labels).astype(F32)
    grad_three = ((probability - onehot) * LOSS_SCALE).astype(BF16)
    grad_two = (outer_cols(grad_three, w3) * slope_two).astype(BF16)
    return act_two, grad_three, grad_two


def seeds_kernel(place_ref, z_ref, left_ref, counts_ref, labels_ref, w2s_ref, w2n_ref, w3_ref, o_ref, stage):
    mine = pl.ds(pl.multiple_of(place_ref[0] * SEEDS_Y, 8), SEEDS_Y)
    counts = counts_ref[mine, :]
    scale = counts.astype(F32)
    pre_one = z_ref[...].astype(F32)[:ROWS_Y]
    sig_one = sigmoid(pre_one)
    act_one = (pre_one * sig_one).astype(BF16)
    slope_one = sig_one * (1.0 + pre_one * (1.0 - sig_one))
    behind = lax.broadcasted_iota(jnp.int32, (SEEDS_Y, ROWS_Y), 1) - KEEP * lax.broadcasted_iota(jnp.int32, (SEEDS_Y, ROWS_Y), 0)

    def choose(mask):
        return jnp.where(mask, 1.0, 0.0).astype(BF16)

    kept = choose((behind > 0) & (behind <= counts))
    belongs = choose((behind >= 0) & (behind < KEEP))
    is_head = choose(behind == 0)
    head = jnp.dot(is_head, act_one, preferred_element_type=F32).astype(BF16)
    mean_two = (jnp.dot(kept, act_one, preferred_element_type=F32) / scale).astype(BF16)
    _, _, grad_two = top(head, mean_two, labels_ref[mine, :], w2s_ref[...], w2n_ref[...], w3_ref[...])
    ones = jnp.ones((SEEDS_Y, H), BF16)
    grad_rows = inner_rows(belongs, grad_two).astype(BF16)
    scale_rows = inner_rows(belongs, (ones * scale).astype(BF16))
    grad_mean = outer_cols(grad_rows, w2n_ref[...]) / scale_rows
    grad = jnp.where(inner_rows(kept, ones) > 0.5, grad_mean, 0.0)
    grad = jnp.where(inner_rows(is_head, ones) > 0.5, outer_cols(grad_rows, w2s_ref[...]), grad)
    grad_one = inner_rows(left_ref[...], (grad * slope_one).astype(BF16))
    for y in range(Y):
        stage[pl.ds(y * BACK, 32), :] = grad_one[y * 32 :][:32]
        stage[pl.ds(y * BACK + 32, SEEDS_Y), :] = head.astype(F32)
        stage[pl.ds(y * BACK + 32 + SEEDS_Y, SEEDS_Y), :] = mean_two.astype(F32)
    o_ref[...] = stage[...].astype(BF16)


def seeds(place, pre_one, left, counts, labels, w2_self, w2_nbr, w3):
    return pl.pallas_call(
        seeds_kernel,
        out_shape=jax.ShapeDtypeStruct((Y * BACK, H), BF16),
        in_specs=[SMEM] + [VMEM] * 7,
        out_specs=VMEM,
        scratch_shapes=[pltpu.VMEM((Y * BACK, H), F32)],
        compiler_params=pltpu.CompilerParams(vmem_limit_bytes=32 * 1024 * 1024),
        name="seeds",
    )(place, pre_one, left, counts, labels, w2_self, w2_nbr, w3)


def weights_kernel(r_ref, labels_ref, w2s_ref, w2n_ref, w3_ref, o_ref):
    rows = r_ref[...].astype(F32)
    grad_one = jnp.zeros((32, H), F32)
    head, mean_two = [], []
    for y in range(Y):
        grad_one = grad_one + rows[y * BACK :][:32]
        head.append(rows[y * BACK + 32 :][:SEEDS_Y])
        mean_two.append(rows[y * BACK + 32 + SEEDS_Y :][:SEEDS_Y])
    head = jnp.concatenate(head, 0).astype(BF16)
    mean_two = jnp.concatenate(mean_two, 0).astype(BF16)
    act_two, grad_three, grad_two = top(head, mean_two, labels_ref[...], w2s_ref[...], w2n_ref[...], w3_ref[...])
    o_ref[pl.ds(0, H), :] = inner_rows(head, grad_two).astype(BF16)
    o_ref[pl.ds(H, H), :] = inner_rows(mean_two, grad_two).astype(BF16)
    o_ref[pl.ds(2 * H, H), :] = jnp.zeros((H, H), BF16)
    o_ref[pl.ds(2 * H, H), :C] = inner_rows(act_two, grad_three).astype(BF16)
    rest = BATCH * PART - 3 * H
    o_ref[pl.ds(3 * H, rest), :] = jnp.concatenate([grad_one, jnp.zeros((rest - 32, H), F32)], 0).astype(BF16)


def weights(received, labels, w2_self, w2_nbr, w3):
    return pl.pallas_call(
        weights_kernel,
        out_shape=jax.ShapeDtypeStruct((BATCH * PART, H), BF16),
        in_specs=[VMEM] * 5,
        out_specs=VMEM,
        compiler_params=pltpu.CompilerParams(vmem_limit_bytes=32 * 1024 * 1024),
        name="weights",
    )(received, labels, w2_self, w2_nbr, w3)


def exchange(rows, axis, parts):
    received = lax.all_to_all(rows.reshape(parts, -1, rows.shape[1]), axis, 0, 0)
    return received.reshape(rows.shape)


def local(features, nbr_ids, nbr_counts, self_ids, seed_counts, labels, w1_self, w1_nbr, w2_self, w2_nbr, w3):
    packed = gather(self_ids[None], nbr_ids.T, nbr_counts[None], features, w1_self, w1_nbr)
    shares, left = project(exchange(packed, "y", Y))
    pre_one = exchange(spread(exchange(shares, "z", Z)), "z", Z)
    place = lax.axis_index("y").astype(jnp.int32)[None]
    labels = labels[:, None]
    back = seeds(place, pre_one, left, seed_counts[:, None], labels, w2_self, w2_nbr, w3)
    grads = weights(exchange(back, "y", Y), labels, w2_self, w2_nbr, w3)
    grads = lax.all_to_all(grads.reshape(BATCH, PART, H), ("x", "core"), 0, 0)
    summed = jnp.sum(grads.astype(F32), axis=0)
    whole = lax.all_gather(summed, ("x", "core"), axis=0, tiled=True)
    first = 3 * H
    return (
        whole[first : first + COLS],
        whole[first + 16 : first + 16 + COLS],
        whole[:H],
        whole[H : 2 * H],
        whole[2 * H : 3 * H, :C],
    )


def solution(mesh):
    split = Mesh(mesh.devices.reshape(Z, Y, X, CORE), ("z", "y", "x", "core"))
    feat, batch = P(("z", "y"), None), P(("x", "core"))
    in_specs = (feat, P(("x", "core"), None), batch, batch, batch, batch, feat, feat, P(), P(), P())
    out_specs = (feat, feat, P(), P(), P())
    return jax.shard_map(local, mesh=split, in_specs=in_specs, out_specs=out_specs, check_vma=False)
```

time: 198 us -> 145 us (0.73)
  waiting for transfers between devices: 41 us -> 10.9 us
  between operations: 14.2 us -> 0.75 us
  Pallas kernels: 44.4 us -> 31.8 us
  blocking collectives: 80.5 us -> 89.1 us
  starting transfers between devices: 6.15 us -> 3.52 us
    all_to_all x1, waiting for transfers between devices: 41 us -> 10.9 us  [exchange(): lax.all_to_all(rows.reshape(parts, -1, rows.shape[1]), axis, 0, 0)]
    pallas_call x3 -> x5, Pallas kernels: 44.4 us -> 31.8 us  [the longest x1 27.4 us: gather(): pl.pallas_call(gather_kernel, out_shape=jax.ShapeDtypeStruct((Y * SEND, 1...]
    all_to_all x3 -> x4, blocking collectives: 66.2 us -> 74.8 us  [the longest x3 56.5 us: exchange(): lax.all_to_all(rows.reshape(parts, -1, rows.shape[1]), axis, 0, 0)]
    all_to_all x1, starting transfers between devices: 6.11 us -> 3.52 us  [exchange(): lax.all_to_all(rows.reshape(parts, -1, rows.shape[1]), axis, 0, 0)]
    concatenate x5 -> x0, local copies, waits for them, and re-layouts: 2.45 us -> none  [the longest x4 2.37 us: local(): jnp.concatenate([self_ids[:, None], jnp.where(valid, nbr_ids, NODES)], 1)]
    unnamed x18 -> x20, local copies, waits for them, and re-layouts: 3.15 us -> 4.79 us
  transfers between devices with their start and end apart: 2 -> 1, of which waited for: 1 -> 1; matrix products, arithmetic and copies ran while one was open for 2% -> 0% of each run, Pallas kernels for 21% -> 0%
where the time goes in v2:
time: 145 us; the launch traced here: 144 us
  blocking collectives  89.1 us (61%)
  Pallas kernels  31.8 us (22%)
  waiting for transfers between devices  10.9 us (8%)
  local copies, waits for them, and re-layouts  7.91 us (5%)
  starting transfers between devices  3.52 us (2%)
    all_to_all x3, blocking collectives, exchange(): lax.all_to_all(rows.reshape(parts, -1, rows.shape[1]), axis, 0, 0)  56.5 us
    pallas_call x1, Pallas kernels, gather(): pl.pallas_call(gather_kernel, out_shape=jax.ShapeDtypeStruct((Y * SEND, 1...  27.4 us
    all_to_all x1, blocking collectives, local(): grads = lax.all_to_all(grads.reshape(BATCH, PART, H), ('x', 'core'), 0, 0)  18.2 us
    all_gather x1, blocking collectives, local(): whole = lax.all_gather(summed, ('x', 'core'), axis=0, tiled=True)  14.3 us
    all_to_all x1, waiting for transfers between devices, exchange(): lax.all_to_all(rows.reshape(parts, -1, rows.shape[1]), axis, 0, 0)  10.9 us
    unnamed x20, local copies, waits for them, and re-layouts  4.79 us
    all_to_all x1, starting transfers between devices, exchange(): lax.all_to_all(rows.reshape(parts, -1, rows.shape[1]), axis, 0, 0)  3.52 us
  transfers between devices with their start and end apart: 1, of which 1 were waited for; matrix products, arithmetic and copies ran while one was open for 0% of the time, Pallas kernels for 0%

profile of v2, /device:TPU:1, one launch (start us, length us, event | category | flops | bytes accessed | tf_op | source)
XLA Modules:
  0.0 144.0 jit_solution(2916806145346502727)
XLA Ops:
  0.6 0.7 broadcast_in_dim.16.self_ref
  1.3 0.7 broadcast_in_dim.17.counts_ref
  2.1 1.6 %copy-done = bf16[11,65536]{1,0:T(8,128)(2,1)S(1)} copy-done((bf16[11,65536]{1,0:T(8,128)(2,1)S(1)}, bf16[11,65536]{1,0:T(8,128)(2,1)}, u32[]{:S(2)}) %copy-start) | copy-done | bytes 1441816
  3.7 0.9 copy-done.3
  4.6 0.7 copy-done.4
  5.3 0.7 copy-done.5
  6.0 27.4 %gather.1 = bf16[1152,128]{1,0:T(8,128)(2,1)S(1)} custom-call(s32[1,2112]{1,0:T(1,128)S(1)} %broadcast_in_dim.16.self_ref, s32[15,2112]{1,0:T(8,128)S(1)} %bitcast.20, s32[1,2112]{1,0:T(1,128)S(1)} %broadcast_in_dim.17.counts_ref, bf16[11,65536]{1,0:T(8,128)(2,1)S(1)} %copy-done, bf16[11,256]{1,0:T(8,128)(2,1)S(1)} %copy-done.4, bf16[11,256]{1,0:T(8,128)(2,1)S(1)} %copy-done.5), custom_call_target="tpu_custom_call" | custom-call | tf_op jit(solution)/shard_map/gather/pallas_call | solution.py:129
  33.4 17.1 %all_to_all.25 = bf16[8,144,128]{2,1,0:T(8,128)(2,1)S(1)} all-to-all(bf16[8,144,128]{2,1,0:T(8,128)(2,1)S(1)} %bitcast.16), channel_id=1, replica_groups=mesh['z'=12,'y'=8,'x'=4,'core'=2] {'y'}, dimensions={0} | all-to-all | bytes 589824 | tf_op jit(solution)/shard_map/all_to_all | solution.py:308
  50.5 0.3 project.1
  50.8 26.7 %all_to_all.26 = bf16[12,24,256]{2,1,0:T(8,128)(2,1)} all-to-all(bf16[12,24,256]{2,1,0:T(8,128)(2,1)S(1)} %bitcast.19), channel_id=1, replica_groups=mesh['z'=12,'y'=8,'x'=4,'core'=2] {'z'}, dimensions={0} | all-to-all | bytes 294912 | tf_op jit(solution)/shard_map/all_to_all | solution.py:308
  77.5 1.6 %spread.1 = bf16[288,256]{1,0:T(8,128)(2,1)} custom-call(bf16[288,256]{1,0:T(8,128)(2,1)} %bitcast.22), custom_call_target="tpu_custom_call" | custom-call | tf_op jit(solution)/shard_map/spread/pallas_call | solution.py:197
  79.1 3.5 %all-to-all-start.2 = ((bf16[12,24,256]{2,1,0:T(8,128)(2,1)}), bf16[12,24,256]{2,1,0:T(8,128)(2,1)S(1)}, u32[]{:S(2)}, u32[]{:S(2)}) async-start(bf16[12,24,256]{2,1,0:T(8,128)(2,1)} %bitcast.21), calls=%async_computation.2 | async-start | bytes 294912 | tf_op jit(solution)/shard_map/all_to_all | solution.py:308
  82.6 0.1 copy.33.w3_ref
  82.8 0.1 copy.32.labels_ref
  82.9 0.1 copy.31.counts_ref
  83.0 10.9 %all-to-all-done.2 = bf16[12,24,256]{2,1,0:T(8,128)(2,1)S(1)} async-done(((bf16[12,24,256]{2,1,0:T(8,128)(2,1)}), bf16[12,24,256]{2,1,0:T(8,128)(2,1)S(1)}, u32[]{:S(2)}, u32[]{:S(2)}) %all-to-all-start.2) | async-done | bytes 147488 | tf_op jit(solution)/shard_map/all_to_all | solution.py:308
  93.9 1.5 %seeds.1 = bf16[640,256]{1,0:T(8,128)(2,1)S(1)} custom-call(s32[1]{0:T(128)} %bitcast.place_ref, bf16[288,256]{1,0:T(8,128)(2,1)S(1)} %bitcast.18, bf16[264,256]{1,0:T(8,128)(2,1)S(1)} %get-tuple-element.8.left_ref, s32[192,1]{1,0:T(8,128)S(1)} %copy.31.counts_ref, s32[192,1]{1,0:T(8,128)S(1)} %copy.32.labels_ref, bf16[256,256]{1,0:T(8,128)(2,1)S(1)} %copy-done.1, ...), custom_call_target="tpu_custom_call" | custom-call | tf_op jit(solution)/shard_map/seeds/pallas_call | solution.py:266
  95.4 12.7 %all_to_all.27 = bf16[8,80,256]{2,1,0:T(8,128)(2,1)S(1)} all-to-all(bf16[8,80,256]{2,1,0:T(8,128)(2,1)S(1)} %bitcast.14), channel_id=1, replica_groups=mesh['z'=12,'y'=8,'x'=4,'core'=2] {'y'}, dimensions={0} | all-to-all | bytes 655360 | tf_op jit(solution)/shard_map/all_to_all | solution.py:308
  108.1 1.0 weights.1
  109.1 18.2 %all_to_all.28 = bf16[8,104,256]{2,1,0:T(8,128)(2,1)S(1)} all-to-all(bf16[8,104,256]{2,1,0:T(8,128)(2,1)S(1)} %bitcast.13), channel_id=1, replica_groups=mesh['z'=12,'y'=8,'x'=4,'core'=2] {'x','core'}, dimensions={0} | all-to-all | bytes 851968 | tf_op jit(solution)/shard_map/all_to_all | solution.py:320
  127.4 14.3 %all_gather.3 = f32[832,256]{1,0:T(8,128)S(1)} all-gather(f32[104,256]{1,0:T(8,128)S(1)} %convert_reduce_fusion), channel_id=1, replica_groups=mesh['z'=12,'y'=8,'x'=4,'core'=2] {'x','core'}, dimensions={0}, use_global_device_ids=true | all-gather | bytes 958464 | tf_op jit(solution)/shard_map/all_gather | solution.py:322
  141.8 0.8 fusion
  142.6 0.6 fusion.1
  143.2 0.8 copy.36
  (16 shorter events, 0.1 us)
Async XLA Ops:
  2.1 1.6 %copy-start = (bf16[11,65536]{1,0:T(8,128)(2,1)S(1)}, bf16[11,65536]{1,0:T(8,128)(2,1)}, u32[]{:S(2)}) copy-start(bf16[11,65536]{1,0:T(8,128)(2,1)} %x_ref.1) | copy-start | bytes 4325380
  3.6 0.9 copy-start.3
  4.6 0.7 copy-start.4
  5.3 0.7 copy-start.5
  6.0 76.7 %copy-start.6 = (bf16[256,172]{0,1:T(8,128)(2,1)S(1)}, bf16[256,172]{0,1:T(8,128)(2,1)}, u32[]{:S(2)}) copy-start(bf16[256,172]{0,1:T(8,128)(2,1)} %param.21) | copy-start | bytes 264196
  6.0 76.8 %copy-start.7 = (s32[192]{0:T(256)S(1)}, s32[192]{0:T(256)}, u32[]{:S(2)}) copy-start(s32[192]{0:T(256)} %param.16) | copy-start | bytes 2308
  6.0 76.9 %copy-start.8 = (s32[192]{0:T(256)S(1)}, s32[192]{0:T(256)}, u32[]{:S(2)}) copy-start(s32[192]{0:T(256)} %param.15) | copy-start | bytes 2308
  6.0 88.0 %copy-start.1 = (bf16[256,256]{1,0:T(8,128)(2,1)S(1)}, bf16[256,256]{1,0:T(8,128)(2,1)}, u32[]{:S(2)}) copy-start(bf16[256,256]{1,0:T(8,128)(2,1)} %w2s_ref.3) | copy-start | bytes 393220
  6.0 87.9 %copy-start.2 = (bf16[256,256]{1,0:T(8,128)(2,1)S(1)}, bf16[256,256]{1,0:T(8,128)(2,1)}, u32[]{:S(2)}) copy-start(bf16[256,256]{1,0:T(8,128)(2,1)} %w2n_ref.3) | copy-start | bytes 393220
  79.1 14.8 %all-to-all-start.2 = ((bf16[12,24,256]{2,1,0:T(8,128)(2,1)}), bf16[12,24,256]{2,1,0:T(8,128)(2,1)S(1)}, u32[]{:S(2)}, u32[]{:S(2)}) async-start(bf16[12,24,256]{2,1,0:T(8,128)(2,1)} %bitcast.21), calls=%async_computation.2 | async-start | bytes 294912 | tf_op jit(solution)/shard_map/all_to_all | solution.py:308

commit v3 on v2

--- a/solution.py
+++ b/solution.py
@@ -24,72 +24,101 @@
 PACKED = ROWS_Y // GROUPS
 SLOTS = 8
 SLOT_ROWS = NODES // SLOTS
-CHUNK = 128
-LANES = -(-ROWS_B // CHUNK) * CHUNK
+CHUNK = 64
+CHUNKS = ROWS_B // CHUNK
+AHEAD = 4
 WIDE = 24
 SEND = 144
 SHARE = 24
 ROWS_Z = Z * SHARE
 BACK = 32 + 2 * SEEDS_Y
-PART = 104
+AT_FIRST = 2 * H
+AT_THIRD = AT_FIRST + 32
+HALF = 368
+PIECES = 4
 BF16 = jnp.bfloat16
 F32 = jnp.float32
 VMEM = pl.BlockSpec(memory_space=pltpu.VMEM)
 SMEM = pl.BlockSpec(memory_space=pltpu.SMEM)
-
-
-def gather_kernel(self_ref, nbr_ref, counts_ref, x_ref, w1s_ref, w1n_ref, o_ref, table, own_ref, agg_ref, stage, ids, near, sems):
+HBM = pl.BlockSpec(memory_space=pltpu.HBM)
+
+
+def gather_kernel(
+    self_in, nbr_in, counts_in, x_in, w1s_in, w1n_in, o_ref,
+    self_ref, nbr_ref, counts_ref, x_ref, w1s_ref, w1n_ref, small_sems, x_sems,
+    table, own_ref, agg_ref, stage, ids, near, sems,
+):
     lane = lax.broadcasted_iota(jnp.int32, (1, 128), 1)
-
+    small = [(self_in, self_ref), (nbr_in, nbr_ref), (counts_in, counts_ref), (w1s_in, w1s_ref), (w1n_in, w1n_ref)]
+    small = [pltpu.make_async_copy(source, target, small_sems.at[i]) for i, (source, target) in enumerate(small)]
+    for copy in small:
+        copy.start()
+    pieces = []
+    for piece in range(PIECES):
+        pieces.append([])
+        for slot in range(SLOTS):
+            place = pl.ds(slot * SLOT_ROWS + piece * (SLOT_ROWS // PIECES), SLOT_ROWS // PIECES)
+            pieces[piece].append(pltpu.make_async_copy(x_in.at[:, place], x_ref.at[:, place], x_sems.at[piece, slot]))
+            pieces[piece][slot].start()
     def fetch(chunk, slot):
-        at = chunk * CHUNK if isinstance(chunk, int) else pl.multiple_of(chunk * CHUNK, CHUNK)
-        return pltpu.make_async_copy(ids.at[:, pl.ds(at, CHUNK)], near[slot], sems.at[slot])
-
-    last = LANES - CHUNK
-    ids[:, pl.ds(last, CHUNK)] = jnp.zeros((IDS, CHUNK), jnp.int32)
-    valid = lax.broadcasted_iota(jnp.int32, (FAN1, ROWS_B), 0) < counts_ref[...]
-    ids[pl.ds(0, FAN1), pl.ds(0, ROWS_B)] = jnp.where(valid, nbr_ref[...], NODES)
-    ids[pl.ds(FAN1, 1), pl.ds(0, ROWS_B)] = self_ref[...]
-    for slot in range(2):
+        return pltpu.make_async_copy(ids.at[chunk], near[slot], sems.at[slot])
+
+    def tabulate(piece):
+        for copy in pieces[piece]:
+            copy.wait()
+
+        @pl.loop(0, SLOT_ROWS // PIECES // 128, unroll=4)
+        def _(step):
+            block = step + piece * (SLOT_ROWS // PIECES // 128)
+            stacked = []
+            for slot in range(SLOTS):
+                start = pl.multiple_of(slot * SLOT_ROWS + block * 128, 128)
+                stacked += [x_ref[:, pl.ds(start, 128)].astype(F32), jnp.ones((1, 128), F32), jnp.zeros((4, 128), F32)]
+            turned = jnp.concatenate(stacked, 0).astype(BF16).T.astype(F32)
+            for slot in range(SLOTS):
+                start = pl.multiple_of(slot * SLOT_ROWS + block * 128, 128)
+                table[pl.ds(start, 128), :] = jnp.where(lane // 16 == slot, turned, 0.0)
+
+    tabulate(0)
+    for copy in small:
+        copy.wait()
+    counts = counts_ref[...][None, :]
+    valid = lax.broadcasted_iota(jnp.int32, (FAN1, ROWS_B), 0) < counts
+    both = jnp.concatenate([jnp.where(valid, nbr_ref[...], NODES), self_ref[...][None, :]], 0)
+    both = jnp.concatenate([both, jnp.zeros((IDS, CHUNK), jnp.int32)], 1)
+    for tile in range(-(-ROWS_B // 128)):
+        low, high = both[:8, tile * 128 :][:, :128], both[8:, tile * 128 :][:, :128]
+        ids[2 * tile] = jnp.where(lane < CHUNK, low, pltpu.roll(high, CHUNK, 1))
+        if 2 * tile + 1 < CHUNKS:
+            ids[2 * tile + 1] = jnp.where(lane < CHUNK, pltpu.roll(low, CHUNK, 1), high)
+    for slot in range(AHEAD):
         fetch(slot, slot).start()
-
-    @pl.loop(0, SLOT_ROWS // 128, unroll=2)
-    def _(block):
-        stacked = []
-        for slot in range(SLOTS):
-            start = pl.multiple_of(slot * SLOT_ROWS + block * 128, 128)
-            stacked += [x_ref[:, pl.ds(start, 128)].astype(F32), jnp.ones((1, 128), F32), jnp.zeros((4, 128), F32)]
-        turned = jnp.concatenate(stacked, 0).T
-        for slot in range(SLOTS):
-            start = pl.multiple_of(slot * SLOT_ROWS + block * 128, 128)
-            table[pl.ds(start, 128), :] = jnp.where(lane // 16 == slot, turned, 0.0)
-
+    for piece in range(1, PIECES):
+        tabulate(piece)
     table[pl.ds(NODES, 8), :] = jnp.zeros((8, 128), F32)
 
-    def take(chunk, slot, targets):
+    def take(chunk, slot):
+        fetch(chunk, slot).wait()
         first = chunk * CHUNK
-        for i in range(targets):
-            own_ref[pl.ds(first + i, 1), :] = table[pl.ds(near[slot][FAN1, i], 1), :]
-            terms = [table[pl.ds(near[slot][j, i], 1), :] for j in range(FAN1)]
-            while len(terms) > 1:
-                terms = [sum(terms[a : a + 2]) for a in range(0, len(terms), 2)]
-            agg_ref[pl.ds(first + i, 1), :] = terms[0]
-
-    whole = ROWS_B // CHUNK
-
-    @pl.loop(0, whole // 2)
-    def _(pair):
-        for slot in range(2):
-            chunk = pair * 2 + slot
-            fetch(chunk, slot).wait()
-            take(chunk, slot, CHUNK)
-
-            @pl.when(chunk + 2 <= whole)
+        for i in range(CHUNK):
+            rows = [table[pl.ds(near[slot][j % 8, j // 8 * CHUNK + i], 1), :] for j in range(IDS)]
+            own_ref[pl.ds(first + i, 1), :] = rows.pop()
+            while len(rows) > 1:
+                rows = [sum(rows[a : a + 2]) for a in range(0, len(rows), 2)]
+            agg_ref[pl.ds(first + i, 1), :] = rows[0]
+
+    @pl.loop(0, CHUNKS // AHEAD)
+    def _(turn):
+        for slot in range(AHEAD):
+            chunk = turn * AHEAD + slot
+            take(chunk, slot)
+
+            @pl.when(chunk + AHEAD < CHUNKS)
             def _():
-                fetch(chunk + 2, slot).start()
-
-    fetch(whole, 0).wait()
-    take(whole, 0, ROWS_B - whole * CHUNK)
+                fetch(chunk + AHEAD, slot).start()
+
+    for slot in range(CHUNKS % AHEAD):
+        take(CHUNKS // AHEAD * AHEAD + slot, slot)
 
     def halves(low, high, width):
         mask = lane % (2 * width) < width
@@ -129,18 +158,26 @@
     return pl.pallas_call(
         gather_kernel,
         out_shape=jax.ShapeDtypeStruct((Y * SEND, 128), BF16),
-        in_specs=[VMEM] * 6,
+        in_specs=[HBM] * 6,
         out_specs=VMEM,
         scratch_shapes=[
+            pltpu.VMEM((ROWS_B,), jnp.int32),
+            pltpu.VMEM((FAN1, ROWS_B), jnp.int32),
+            pltpu.VMEM((ROWS_B,), jnp.int32),
+            pltpu.VMEM((COLS, NODES), BF16),
+            pltpu.VMEM((COLS, H), BF16),
+            pltpu.VMEM((COLS, H), BF16),
+            pltpu.SemaphoreType.DMA((5,)),
+            pltpu.SemaphoreType.DMA((PIECES, SLOTS)),
             pltpu.VMEM((NODES + 8, 128), F32),
             pltpu.VMEM((ROWS_B, 128), F32),
             pltpu.VMEM((ROWS_B, 128), F32),
             pltpu.VMEM((Y * SEND, 128), F32),
-            pltpu.VMEM((IDS, LANES), jnp.int32),
-            [pltpu.SMEM((IDS, CHUNK), jnp.int32)] * 2,
-            pltpu.SemaphoreType.DMA((2,)),
+            pltpu.VMEM((CHUNKS, 8, 128), jnp.int32),
+            [pltpu.SMEM((8, 128), jnp.int32)] * AHEAD,
+            pltpu.SemaphoreType.DMA((AHEAD,)),
         ],
-        compiler_params=pltpu.CompilerParams(vmem_limit_bytes=50 * 1024 * 1024),
+        compiler_params=pltpu.CompilerParams(vmem_limit_bytes=63 * 1024 * 1024),
         name="gather",
     )(self_ids, nbr_ids, counts, features, w1_self, w1_nbr)
 
@@ -199,6 +236,7 @@
         out_shape=jax.ShapeDtypeStruct((ROWS_Z, H), BF16),
         in_specs=[VMEM],
         out_specs=VMEM,
+        compiler_params=pltpu.CompilerParams(vmem_limit_bytes=16 * 1024 * 1024),
         name="spread",
     )(shares)
 
@@ -220,18 +258,25 @@
     sig_two = sigmoid(pre_two)
     act_two = (pre_two * sig_two).astype(BF16)
     slope_two = sig_two * (1.0 + pre_two * (1.0 - sig_two))
-    logits = jnp.dot(act_two, w3, preferred_element_type=F32)
+    logits = outer_cols(act_two, w3)
     expsum = jnp.exp(logits - jnp.max(logits, axis=1, keepdims=True))
     probability = expsum / jnp.sum(expsum, axis=1, keepdims=True)
     onehot = (lax.broadcasted_iota(jnp.int32, logits.shape, 1) == labels).astype(F32)
     grad_three = ((probability - onehot) * LOSS_SCALE).astype(BF16)
-    grad_two = (outer_cols(grad_three, w3) * slope_two).astype(BF16)
+    grad_two = (jnp.dot(grad_three, w3, preferred_element_type=F32) * slope_two).astype(BF16)
     return act_two, grad_three, grad_two
 
 
+def as_column(ref, first, rows):
+    row = lax.broadcasted_iota(jnp.int32, (rows, SEEDS_B), 0) + first
+    column = lax.broadcasted_iota(jnp.int32, (rows, SEEDS_B), 1)
+    spread_out = jnp.where(row == column, ref[...][None, :], 0).astype(F32)
+    return jnp.sum(spread_out, axis=1, keepdims=True).astype(jnp.int32)
+
+
 def seeds_kernel(place_ref, z_ref, left_ref, counts_ref, labels_ref, w2s_ref, w2n_ref, w3_ref, o_ref, stage):
-    mine = pl.ds(pl.multiple_of(place_ref[0] * SEEDS_Y, 8), SEEDS_Y)
-    counts = counts_ref[mine, :]
+    first = place_ref[0] * SEEDS_Y
+    counts = as_column(counts_ref, first, SEEDS_Y)
     scale = counts.astype(F32)
     pre_one = z_ref[...].astype(F32)[:ROWS_Y]
     sig_one = sigmoid(pre_one)
@@ -247,7 +292,7 @@
     is_head = choose(behind == 0)
     head = jnp.dot(is_head, act_one, preferred_element_type=F32).astype(BF16)
     mean_two = (jnp.dot(kept, act_one, preferred_element_type=F32) / scale).astype(BF16)
-    _, _, grad_two = top(head, mean_two, labels_ref[mine, :], w2s_ref[...], w2n_ref[...], w3_ref[...])
+    _, _, grad_two = top(head, mean_two, as_column(labels_ref, first, SEEDS_Y), w2s_ref[...], w2n_ref[...], w3_ref[...])
     ones = jnp.ones((SEEDS_Y, H), BF16)
     grad_rows = inner_rows(belongs, grad_two).astype(BF16)
     scale_rows = inner_rows(belongs, (ones * scale).astype(BF16))
@@ -284,19 +329,19 @@
         mean_two.append(rows[y * BACK + 32 + SEEDS_Y :][:SEEDS_Y])
     head = jnp.concatenate(head, 0).astype(BF16)
     mean_two = jnp.concatenate(mean_two, 0).astype(BF16)
-    act_two, grad_three, grad_two = top(head, mean_two, labels_ref[...], w2s_ref[...], w2n_ref[...], w3_ref[...])
-    o_ref[pl.ds(0, H), :] = inner_rows(head, grad_two).astype(BF16)
-    o_ref[pl.ds(H, H), :] = inner_rows(mean_two, grad_two).astype(BF16)
-    o_ref[pl.ds(2 * H, H), :] = jnp.zeros((H, H), BF16)
-    o_ref[pl.ds(2 * H, H), :C] = inner_rows(act_two, grad_three).astype(BF16)
-    rest = BATCH * PART - 3 * H
-    o_ref[pl.ds(3 * H, rest), :] = jnp.concatenate([grad_one, jnp.zeros((rest - 32, H), F32)], 0).astype(BF16)
+    act_two, grad_three, grad_two = top(head, mean_two, as_column(labels_ref, 0, SEEDS_B), w2s_ref[...], w2n_ref[...], w3_ref[...])
+    o_ref[pl.ds(0, H), :] = inner_rows(head, grad_two)
+    o_ref[pl.ds(H, H), :] = inner_rows(mean_two, grad_two)
+    o_ref[pl.ds(AT_FIRST, 32), :] = grad_one
+    o_ref[pl.ds(AT_THIRD, C), :] = inner_rows(grad_three, act_two)
+    rest = 2 * HALF - AT_THIRD - C
+    o_ref[pl.ds(AT_THIRD + C, rest), :] = jnp.zeros((rest, H), F32)
 
 
 def weights(received, labels, w2_self, w2_nbr, w3):
     return pl.pallas_call(
         weights_kernel,
-        out_shape=jax.ShapeDtypeStruct((BATCH * PART, H), BF16),
+        out_shape=jax.ShapeDtypeStruct((2 * HALF, H), F32),
         in_specs=[VMEM] * 5,
         out_specs=VMEM,
         compiler_params=pltpu.CompilerParams(vmem_limit_bytes=32 * 1024 * 1024),
@@ -304,30 +349,69 @@
     )(received, labels, w2_self, w2_nbr, w3)
 
 
+def halve_kernel(g_ref, o_ref):
+    total = (g_ref[pl.ds(0, HALF), :] + g_ref[pl.ds(HALF, HALF), :]).astype(BF16)
+    for x in range(X):
+        o_ref[pl.ds(x * HALF, HALF), :] = total
+
+
+def halve(received):
+    return pl.pallas_call(
+        halve_kernel,
+        out_shape=jax.ShapeDtypeStruct((X * HALF, H), BF16),
+        in_specs=[VMEM],
+        out_specs=VMEM,
+        compiler_params=pltpu.CompilerParams(vmem_limit_bytes=16 * 1024 * 1024),
+        name="halve",
+    )(received)
+
+
+def finish_kernel(g_ref, w1s_ref, w1n_ref, w2s_ref, w2n_ref, w3_ref, sems):
+    copies = [
+        pltpu.make_async_copy(g_ref.at[pl.ds(0, H), :], w2s_ref, sems.at[0]),
+        pltpu.make_async_copy(g_ref.at[pl.ds(H, H), :], w2n_ref, sems.at[1]),
+    ]
+    for copy in copies:
+        copy.start()
+    first = g_ref[pl.ds(AT_FIRST, 32), :]
+    w1s_ref[...] = first[:COLS]
+    w1n_ref[...] = first[16 : 16 + COLS]
+    w3_ref[...] = g_ref[pl.ds(AT_THIRD, C), :]
+    for copy in copies:
+        copy.wait()
+
+
+def finish(gradients):
+    shapes = [(COLS, H), (COLS, H), (H, H), (H, H), (C, H)]
+    anywhere = pl.BlockSpec(memory_space=pl.ANY)
+    return pl.pallas_call(
+        finish_kernel,
+        out_shape=tuple(jax.ShapeDtypeStruct(shape, F32) for shape in shapes),
+        in_specs=[VMEM],
+        out_specs=(VMEM, VMEM, anywhere, anywhere, VMEM),
+        scratch_shapes=[pltpu.SemaphoreType.DMA((2,))],
+        compiler_params=pltpu.CompilerParams(vmem_limit_bytes=16 * 1024 * 1024),
+        name="finish",
+    )(gradients)
+
+
 def exchange(rows, axis, parts):
     received = lax.all_to_all(rows.reshape(parts, -1, rows.shape[1]), axis, 0, 0)
     return received.reshape(rows.shape)
 
 
 def local(features, nbr_ids, nbr_counts, self_ids, seed_counts, labels, w1_self, w1_nbr, w2_self, w2_nbr, w3):
-    packed = gather(self_ids[None], nbr_ids.T, nbr_counts[None], features, w1_self, w1_nbr)
+    packed = gather(self_ids, nbr_ids.T, nbr_counts, features, w1_self, w1_nbr)
     shares, left = project(exchange(packed, "y", Y))
     pre_one = exchange(spread(exchange(shares, "z", Z)), "z", Z)
     place = lax.axis_index("y").astype(jnp.int32)[None]
-    labels = labels[:, None]
-    back = seeds(place, pre_one, left, seed_counts[:, None], labels, w2_self, w2_nbr, w3)
-    grads = weights(exchange(back, "y", Y), labels, w2_self, w2_nbr, w3)
-    grads = lax.all_to_all(grads.reshape(BATCH, PART, H), ("x", "core"), 0, 0)
-    summed = jnp.sum(grads.astype(F32), axis=0)
-    whole = lax.all_gather(summed, ("x", "core"), axis=0, tiled=True)
-    first = 3 * H
-    return (
-        whole[first : first + COLS],
-        whole[first + 16 : first + 16 + COLS],
-        whole[:H],
-        whole[H : 2 * H],
-        whole[2 * H : 3 * H, :C],
-    )
+    back = seeds(place, pre_one, left, seed_counts, labels, w2_self, w2_nbr, w3.T)
+    grads = weights(exchange(back, "y", Y), labels, w2_self, w2_nbr, w3.T)
+    grads = exchange(halve(exchange(grads, "core", CORE)), "x", X)
+    summed = jnp.sum(grads.reshape(X, HALF, H).astype(F32), axis=0)
+    whole = lax.all_gather(summed, "core", axis=0, tiled=True)
+    grad_w1s, grad_w1n, grad_w2s, grad_w2n, grad_w3 = finish(whole)
+    return grad_w1s, grad_w1n, grad_w2s, grad_w2n, grad_w3.T
 
 
 def solution(mesh):

time: 145 us -> 134 us (0.924)
  local copies, waits for them, and re-layouts: 7.91 us -> 0.02 us
  blocking collectives: 89.1 us -> 85 us
    all_to_all x3 -> x5, blocking collectives: 56.5 us -> 81.3 us  [exchange(): lax.all_to_all(rows.reshape(parts, -1, rows.shape[1]), axis, 0, 0)]
    all_to_all x1 -> x0, blocking collectives: 18.2 us -> none  [local(): grads = lax.all_to_all(grads.reshape(BATCH, PART, H), ('x', 'core'), 0, 0)]
    all_gather x1, blocking collectives: 14.3 us -> 3.7 us  [local(): whole = lax.all_gather(summed, 'core', axis=0, tiled=True)]
    unnamed x20 -> x10, local copies, waits for them, and re-layouts: 4.79 us -> 0.02 us
    broadcast_in_dim x4 -> x0, local copies, waits for them, and re-layouts: 1.66 us -> none  [the longest x1 0.71 us: local(): self_ids[None]]
    pallas_call x1 -> x3, Pallas kernels: 0.99 us -> 2.46 us  [the longest x1 1.49 us: finish(): pl.pallas_call(finish_kernel, out_shape=tuple((jax.ShapeDtypeStruct(shape...]
    slice x3 -> x0, local copies, waits for them, and re-layouts: 1.45 us -> none  [the longest x1 0.82 us: local(): whole[H:2 * H]]
where the time goes in v3:
time: 134 us; the launch traced here: 133 us
  blocking collectives  85 us (63%)
  Pallas kernels  32.7 us (24%)
  waiting for transfers between devices  11.3 us (8%)
  starting transfers between devices  3.52 us (3%)
    all_to_all x5, blocking collectives, exchange(): lax.all_to_all(rows.reshape(parts, -1, rows.shape[1]), axis, 0, 0)  81.3 us
    pallas_call x1, Pallas kernels, gather(): pl.pallas_call(gather_kernel, out_shape=jax.ShapeDtypeStruct((Y * SEND, 1...  27.8 us
    all_to_all x1, waiting for transfers between devices, exchange(): lax.all_to_all(rows.reshape(parts, -1, rows.shape[1]), axis, 0, 0)  11.3 us
    all_gather x1, blocking collectives, local(): whole = lax.all_gather(summed, 'core', axis=0, tiled=True)  3.7 us
    all_to_all x1, starting transfers between devices, exchange(): lax.all_to_all(rows.reshape(parts, -1, rows.shape[1]), axis, 0, 0)  3.52 us
  transfers between devices with their start and end apart: 1, of which 1 were waited for; matrix products, arithmetic and copies ran while one was open for 0% of the time, Pallas kernels for 0%

profile of v3, /device:TPU:1, one launch (start us, length us, event | category | flops | bytes accessed | tf_op | source)
XLA Modules:
  0.0 133.4 jit_solution(5306654897952280163)
XLA Ops:
  0.6 0.0 copy-start
  0.6 0.0 copy-start.1
  0.7 0.0 copy-start.2
  0.7 0.0 copy-start.3
  0.7 0.0 copy-start.4
  0.7 27.8 %gather.1 = bf16[1152,128]{1,0:T(8,128)(2,1)} custom-call(s32[2112]{0:T(1024)} %self_in.1, s32[15,2112]{1,0:T(8,128)} %bitcast.27, s32[2112]{0:T(1024)} %counts_in.1, bf16[11,65536]{1,0:T(8,128)(2,1)} %x_in.1, bf16[11,256]{1,0:T(8,128)(2,1)} %w1s_in.1, bf16[11,256]{1,0:T(8,128)(2,1)} %w1n_in.1), custom_call_target="tpu_custom_call" | custom-call | tf_op jit(solution)/shard_map/gather/pallas_call | solution.py:158
  28.4 17.3 %all_to_all.30 = bf16[8,144,128]{2,1,0:T(8,128)(2,1)S(1)} all-to-all(bf16[8,144,128]{2,1,0:T(8,128)(2,1)} %bitcast.26), channel_id=1, replica_groups=mesh['z'=12,'y'=8,'x'=4,'core'=2] {'y'}, dimensions={0} | all-to-all | bytes 589824 | tf_op jit(solution)/shard_map/all_to_all | solution.py:399
  45.8 0.3 project.1
  46.1 26.6 %all_to_all.31 = bf16[12,24,256]{2,1,0:T(8,128)(2,1)S(1)} all-to-all(bf16[12,24,256]{2,1,0:T(8,128)(2,1)S(1)} %bitcast.25), channel_id=1, replica_groups=mesh['z'=12,'y'=8,'x'=4,'core'=2] {'z'}, dimensions={0} | all-to-all | bytes 294912 | tf_op jit(solution)/shard_map/all_to_all | solution.py:399
  72.7 0.7 spread.1
  73.3 3.5 %all-to-all-start.2 = ((bf16[12,24,256]{2,1,0:T(8,128)(2,1)}), bf16[12,24,256]{2,1,0:T(8,128)(2,1)S(1)}, u32[]{:S(2)}, u32[]{:S(2)}) async-start(bf16[12,24,256]{2,1,0:T(8,128)(2,1)} %bitcast.6), calls=%async_computation.2 | async-start | bytes 294912 | tf_op jit(solution)/shard_map/all_to_all | solution.py:399
  76.9 11.3 %all-to-all-done.2 = bf16[12,24,256]{2,1,0:T(8,128)(2,1)S(1)} async-done(((bf16[12,24,256]{2,1,0:T(8,128)(2,1)}), bf16[12,24,256]{2,1,0:T(8,128)(2,1)S(1)}, u32[]{:S(2)}, u32[]{:S(2)}) %all-to-all-start.2) | async-done | bytes 147488 | tf_op jit(solution)/shard_map/all_to_all | solution.py:399
  88.1 0.0 copy-done
  88.1 0.0 copy-done.1
  88.2 0.0 copy-done.2
  88.2 1.5 %seeds.1 = bf16[640,256]{1,0:T(8,128)(2,1)S(1)} custom-call(s32[1]{0:T(128)} %bitcast.place_ref, bf16[288,256]{1,0:T(8,128)(2,1)S(1)} %bitcast.21, bf16[264,256]{1,0:T(8,128)(2,1)S(1)} %get-tuple-element.13.left_ref, s32[192]{0:T(256)S(1)} %copy-done.4, s32[192]{0:T(256)S(1)} %copy-done.3, bf16[256,256]{1,0:T(8,128)(2,1)S(1)} %copy-done, ...), custom_call_target="tpu_custom_call" | custom-call | tf_op jit(solution)/shard_map/seeds/pallas_call | solution.py:311
  89.7 12.7 %all_to_all.32 = bf16[8,80,256]{2,1,0:T(8,128)(2,1)S(1)} all-to-all(bf16[8,80,256]{2,1,0:T(8,128)(2,1)S(1)} %bitcast.18), channel_id=1, replica_groups=mesh['z'=12,'y'=8,'x'=4,'core'=2] {'y'}, dimensions={0} | all-to-all | bytes 655360 | tf_op jit(solution)/shard_map/all_to_all | solution.py:399
  102.4 0.9 weights.1
  103.3 9.7 %all_to_all.33 = f32[2,368,256]{2,1,0:T(8,128)S(1)} all-to-all(f32[2,368,256]{2,1,0:T(8,128)S(1)} %bitcast.15), channel_id=1, replica_groups=mesh['z'=12,'y'=8,'x'=4,'core'=2] {'core'}, dimensions={0} | all-to-all | bytes 1507328 | tf_op jit(solution)/shard_map/all_to_all | solution.py:399
  113.0 0.1 halve.1
  113.1 15.0 %all_to_all.34 = bf16[4,368,256]{2,1,0:T(8,128)(2,1)S(1)} all-to-all(bf16[4,368,256]{2,1,0:T(8,128)(2,1)S(1)} %bitcast.17), channel_id=1, replica_groups=mesh['z'=12,'y'=8,'x'=4,'core'=2] {'x'}, dimensions={0} | all-to-all | bytes 1507328 | tf_op jit(solution)/shard_map/all_to_all | solution.py:399
  128.1 0.1 convert_reduce_fusion
  128.2 3.7 %all_gather.3.g_ref = f32[736,256]{1,0:T(8,128)S(1)} all-gather(f32[368,256]{1,0:T(8,128)S(1)} %convert_reduce_fusion), channel_id=1, replica_groups=mesh['z'=12,'y'=8,'x'=4,'core'=2] {'core'}, dimensions={0}, use_global_device_ids=true | all-gather | bytes 1130496 | tf_op jit(solution)/shard_map/all_gather | solution.py:412
  131.9 1.5 %finish.1 = (f32[11,256]{1,0:T(8,128)}, f32[11,256]{1,0:T(8,128)}, f32[256,256]{1,0:T(8,128)}, f32[256,256]{1,0:T(8,128)}, f32[172,256]{1,0:T(8,128)}) custom-call(f32[736,256]{1,0:T(8,128)S(1)} %all_gather.3.g_ref), custom_call_target="tpu_custom_call" | custom-call | tf_op jit(solution)/shard_map/finish/pallas_call | solution.py:387
  (2 shorter events, 0.0 us)
Async XLA Ops:
  0.6 87.5 %copy-start = (bf16[256,256]{1,0:T(8,128)(2,1)S(1)}, bf16[256,256]{1,0:T(8,128)(2,1)}, u32[]{:S(2)}) copy-start(bf16[256,256]{1,0:T(8,128)(2,1)} %w2s_ref.3) | copy-start | bytes 393220
  0.6 87.5 %copy-start.1 = (bf16[256,256]{1,0:T(8,128)(2,1)S(1)}, bf16[256,256]{1,0:T(8,128)(2,1)}, u32[]{:S(2)}) copy-start(bf16[256,256]{1,0:T(8,128)(2,1)} %w2n_ref.3) | copy-start | bytes 393220
  0.7 87.5 %copy-start.2 = (bf16[256,172]{0,1:T(8,128)(2,1)S(1)}, bf16[256,172]{0,1:T(8,128)(2,1)}, u32[]{:S(2)}) copy-start(bf16[256,172]{0,1:T(8,128)(2,1)} %param.21) | copy-start | bytes 264196
  0.7 87.5 %copy-start.3 = (s32[192]{0:T(256)S(1)}, s32[192]{0:T(256)}, u32[]{:S(2)}) copy-start(s32[192]{0:T(256)} %labels_ref.3) | copy-start | bytes 2308
  0.7 87.5 %copy-start.4 = (s32[192]{0:T(256)S(1)}, s32[192]{0:T(256)}, u32[]{:S(2)}) copy-start(s32[192]{0:T(256)} %counts_ref.1) | copy-start | bytes 2308
  73.3 14.8 %all-to-all-start.2 = ((bf16[12,24,256]{2,1,0:T(8,128)(2,1)}), bf16[12,24,256]{2,1,0:T(8,128)(2,1)S(1)}, u32[]{:S(2)}, u32[]{:S(2)}) async-start(bf16[12,24,256]{2,1,0:T(8,128)(2,1)} %bitcast.6), calls=%async_computation.2 | async-start | bytes 294912 | tf_op jit(solution)/shard_map/all_to_all | solution.py:399

commit v4 on v3

--- a/solution.py
+++ b/solution.py
@@ -35,7 +35,7 @@
 AT_FIRST = 2 * H
 AT_THIRD = AT_FIRST + 32
 HALF = 368
-PIECES = 4
+PIECES = 2
 BF16 = jnp.bfloat16
 F32 = jnp.float32
 VMEM = pl.BlockSpec(memory_space=pltpu.VMEM)
@@ -46,7 +46,7 @@
 def gather_kernel(
     self_in, nbr_in, counts_in, x_in, w1s_in, w1n_in, o_ref,
     self_ref, nbr_ref, counts_ref, x_ref, w1s_ref, w1n_ref, small_sems, x_sems,
-    table, own_ref, agg_ref, stage, ids, near, sems,
+    table, own_ref, agg_ref, ids, near, sems,
 ):
     lane = lax.broadcasted_iota(jnp.int32, (1, 128), 1)
     small = [(self_in, self_ref), (nbr_in, nbr_ref), (counts_in, counts_ref), (w1s_in, w1s_ref), (w1n_in, w1n_ref)]
@@ -67,7 +67,7 @@
         for copy in pieces[piece]:
             copy.wait()
 
-        @pl.loop(0, SLOT_ROWS // PIECES // 128, unroll=4)
+        @pl.loop(0, SLOT_ROWS // PIECES // 128, unroll=8)
         def _(step):
             block = step + piece * (SLOT_ROWS // PIECES // 128)
             stacked = []
@@ -127,8 +127,15 @@
         moved = jnp.where(mask, pltpu.roll(low, 128 - width, 1), pltpu.roll(high, width, 1))
         return jnp.where(mask, low, high) + moved
 
-    @pl.loop(0, Y)
+    w1 = jnp.concatenate([w1s_ref[...].astype(F32), w1n_ref[...].astype(F32), jnp.zeros((WIDE - 2 * COLS, H), F32)], 0)
+    w1 = [w1[:, :128], w1[:, 128:], jnp.zeros((SEND - PACKED - 2 * WIDE, 128), F32)]
+    row = lax.broadcasted_iota(jnp.int32, (128, 128), 0)
+    column = lax.broadcasted_iota(jnp.int32, (128, 128), 1)
+    counter = jnp.where((row % 16 == COLS) & (row // 16 == column // 16), 1.0, 0.0).astype(BF16)
+
+    @pl.loop(0, Y, unroll=2)
     def _(block):
+        message = []
         for step in range(PACKED // 8):
             v = []
             for group in range(GROUPS):
@@ -136,22 +143,12 @@
                 v += [own_ref[place, :], agg_ref[place, :]]
             v = [halves(v[q], v[q + 4] if q < 2 else None, 64) for q in range(4)]
             v = [halves(v[q], v[q + 2], 32) for q in range(2)]
-            stage[pl.ds(pl.multiple_of(block * SEND + step * 8, 8), 8), :] = halves(v[0], v[1], 16)
-
-    w1 = jnp.concatenate([w1s_ref[...].astype(F32), w1n_ref[...].astype(F32), jnp.zeros((WIDE - 2 * COLS, H), F32)], 0)
-    row = lax.broadcasted_iota(jnp.int32, (128, 128), 0)
-    column = lax.broadcasted_iota(jnp.int32, (128, 128), 1)
-    counter = jnp.where((row % 16 == COLS) & (row // 16 == column // 16), 1.0, 0.0).astype(BF16)
-
-    @pl.loop(0, Y)
-    def _(block):
-        first = pl.multiple_of(block * SEND, 16)
-        packed = stage[pl.ds(first, PACKED), :]
+            message.append(halves(v[0], v[1], 16))
+        packed = jnp.concatenate(message, 0)
         counted = jnp.dot(packed.astype(BF16), counter, preferred_element_type=F32)
         packed = jnp.where((lane < GROUPS * 32) & (lane % 16 < COLS), packed / counted, 0.0)
-        rest = jnp.zeros((SEND - PACKED - 2 * WIDE, 128), F32)
-        message = jnp.concatenate([packed, w1[:, :128], w1[:, 128:], rest], 0)
-        o_ref[pl.ds(first, SEND), :] = message.astype(BF16)
+        message = jnp.concatenate([packed] + w1, 0).astype(BF16)
+        o_ref[pl.ds(pl.multiple_of(block * SEND, 16), SEND), :] = message
 
 
 def gather(self_ids, nbr_ids, counts, features, w1_self, w1_nbr):
@@ -172,7 +169,6 @@
             pltpu.VMEM((NODES + 8, 128), F32),
             pltpu.VMEM((ROWS_B, 128), F32),
             pltpu.VMEM((ROWS_B, 128), F32),
-            pltpu.VMEM((Y * SEND, 128), F32),
             pltpu.VMEM((CHUNKS, 8, 128), jnp.int32),
             [pltpu.SMEM((8, 128), jnp.int32)] * AHEAD,
             pltpu.SemaphoreType.DMA((AHEAD,)),

time: 134 us -> 132 us (0.985)
  Pallas kernels: 32.7 us -> 30.9 us
    pallas_call x1, Pallas kernels: 27.8 us -> 25.9 us  [gather(): pl.pallas_call(gather_kernel, out_shape=jax.ShapeDtypeStruct((Y * SEND, 1...]
where the time goes in v4:
time: 132 us
  blocking collectives  85 us (64%)
  Pallas kernels  30.9 us (23%)
  waiting for transfers between devices  11.3 us (9%)
  starting transfers between devices  3.52 us (3%)
    all_to_all x5, blocking collectives, exchange(): lax.all_to_all(rows.reshape(parts, -1, rows.shape[1]), axis, 0, 0)  81.3 us
    pallas_call x1, Pallas kernels, gather(): pl.pallas_call(gather_kernel, out_shape=jax.ShapeDtypeStruct((Y * SEND, 1...  25.9 us
    all_to_all x1, waiting for transfers between devices, exchange(): lax.all_to_all(rows.reshape(parts, -1, rows.shape[1]), axis, 0, 0)  11.3 us
    all_gather x1, blocking collectives, local(): whole = lax.all_gather(summed, 'core', axis=0, tiled=True)  3.7 us
    all_to_all x1, starting transfers between devices, exchange(): lax.all_to_all(rows.reshape(parts, -1, rows.shape[1]), axis, 0, 0)  3.52 us
  transfers between devices with their start and end apart: 1, of which 1 were waited for; matrix products, arithmetic and copies ran while one was open for 0% of the time, Pallas kernels for 0%

profile of v4, /device:TPU:1, one launch (start us, length us, event | category | flops | bytes accessed | tf_op | source)
XLA Modules:
  0.0 131.6 jit_solution(13943220400488047288)
XLA Ops:
  0.6 0.0 copy-start
  0.6 0.0 copy-start.1
  0.7 0.0 copy-start.2
  0.7 0.0 copy-start.3
  0.7 0.0 copy-start.4
  0.7 25.9 %gather.1 = bf16[1152,128]{1,0:T(8,128)(2,1)} custom-call(s32[2112]{0:T(1024)} %self_in.1, s32[15,2112]{1,0:T(8,128)} %bitcast.27, s32[2112]{0:T(1024)} %counts_in.1, bf16[11,65536]{1,0:T(8,128)(2,1)} %x_in.1, bf16[11,256]{1,0:T(8,128)(2,1)} %w1s_in.1, bf16[11,256]{1,0:T(8,128)(2,1)} %w1n_in.1), custom_call_target="tpu_custom_call" | custom-call | tf_op jit(solution)/shard_map/gather/pallas_call | solution.py:155
  26.6 17.3 %all_to_all.30 = bf16[8,144,128]{2,1,0:T(8,128)(2,1)S(1)} all-to-all(bf16[8,144,128]{2,1,0:T(8,128)(2,1)} %bitcast.26), channel_id=1, replica_groups=mesh['z'=12,'y'=8,'x'=4,'core'=2] {'y'}, dimensions={0} | all-to-all | bytes 589824 | tf_op jit(solution)/shard_map/all_to_all | solution.py:395
  44.0 0.3 project.1
  44.3 26.6 %all_to_all.31 = bf16[12,24,256]{2,1,0:T(8,128)(2,1)S(1)} all-to-all(bf16[12,24,256]{2,1,0:T(8,128)(2,1)S(1)} %bitcast.25), channel_id=1, replica_groups=mesh['z'=12,'y'=8,'x'=4,'core'=2] {'z'}, dimensions={0} | all-to-all | bytes 294912 | tf_op jit(solution)/shard_map/all_to_all | solution.py:395
  70.8 0.7 spread.1
  71.5 3.5 %all-to-all-start.2 = ((bf16[12,24,256]{2,1,0:T(8,128)(2,1)}), bf16[12,24,256]{2,1,0:T(8,128)(2,1)S(1)}, u32[]{:S(2)}, u32[]{:S(2)}) async-start(bf16[12,24,256]{2,1,0:T(8,128)(2,1)} %bitcast.6), calls=%async_computation.2 | async-start | bytes 294912 | tf_op jit(solution)/shard_map/all_to_all | solution.py:395
  75.1 11.3 %all-to-all-done.2 = bf16[12,24,256]{2,1,0:T(8,128)(2,1)S(1)} async-done(((bf16[12,24,256]{2,1,0:T(8,128)(2,1)}), bf16[12,24,256]{2,1,0:T(8,128)(2,1)S(1)}, u32[]{:S(2)}, u32[]{:S(2)}) %all-to-all-start.2) | async-done | bytes 147488 | tf_op jit(solution)/shard_map/all_to_all | solution.py:395
  86.3 0.0 copy-done
  86.3 0.0 copy-done.1
  86.3 0.0 copy-done.2
  86.4 1.5 %seeds.1 = bf16[640,256]{1,0:T(8,128)(2,1)S(1)} custom-call(s32[1]{0:T(128)} %bitcast.place_ref, bf16[288,256]{1,0:T(8,128)(2,1)S(1)} %bitcast.21, bf16[264,256]{1,0:T(8,128)(2,1)S(1)} %get-tuple-element.13.left_ref, s32[192]{0:T(256)S(1)} %copy-done.4, s32[192]{0:T(256)S(1)} %copy-done.3, bf16[256,256]{1,0:T(8,128)(2,1)S(1)} %copy-done, ...), custom_call_target="tpu_custom_call" | custom-call | tf_op jit(solution)/shard_map/seeds/pallas_call | solution.py:307
  87.9 12.7 %all_to_all.32 = bf16[8,80,256]{2,1,0:T(8,128)(2,1)S(1)} all-to-all(bf16[8,80,256]{2,1,0:T(8,128)(2,1)S(1)} %bitcast.18), channel_id=1, replica_groups=mesh['z'=12,'y'=8,'x'=4,'core'=2] {'y'}, dimensions={0} | all-to-all | bytes 655360 | tf_op jit(solution)/shard_map/all_to_all | solution.py:395
  100.6 0.9 weights.1
  101.5 9.7 %all_to_all.33 = f32[2,368,256]{2,1,0:T(8,128)S(1)} all-to-all(f32[2,368,256]{2,1,0:T(8,128)S(1)} %bitcast.15), channel_id=1, replica_groups=mesh['z'=12,'y'=8,'x'=4,'core'=2] {'core'}, dimensions={0} | all-to-all | bytes 1507328 | tf_op jit(solution)/shard_map/all_to_all | solution.py:395
  111.2 0.1 halve.1
  111.3 15.0 %all_to_all.34 = bf16[4,368,256]{2,1,0:T(8,128)(2,1)S(1)} all-to-all(bf16[4,368,256]{2,1,0:T(8,128)(2,1)S(1)} %bitcast.17), channel_id=1, replica_groups=mesh['z'=12,'y'=8,'x'=4,'core'=2] {'x'}, dimensions={0} | all-to-all | bytes 1507328 | tf_op jit(solution)/shard_map/all_to_all | solution.py:395
  126.3 0.1 convert_reduce_fusion
  126.4 3.7 %all_gather.3.g_ref = f32[736,256]{1,0:T(8,128)S(1)} all-gather(f32[368,256]{1,0:T(8,128)S(1)} %convert_reduce_fusion), channel_id=1, replica_groups=mesh['z'=12,'y'=8,'x'=4,'core'=2] {'core'}, dimensions={0}, use_global_device_ids=true | all-gather | bytes 1130496 | tf_op jit(solution)/shard_map/all_gather | solution.py:408
  130.1 1.5 %finish.1 = (f32[11,256]{1,0:T(8,128)}, f32[11,256]{1,0:T(8,128)}, f32[256,256]{1,0:T(8,128)}, f32[256,256]{1,0:T(8,128)}, f32[172,256]{1,0:T(8,128)}) custom-call(f32[736,256]{1,0:T(8,128)S(1)} %all_gather.3.g_ref), custom_call_target="tpu_custom_call" | custom-call | tf_op jit(solution)/shard_map/finish/pallas_call | solution.py:383
  (2 shorter events, 0.0 us)
Async XLA Ops:
  0.6 85.7 %copy-start = (bf16[256,256]{1,0:T(8,128)(2,1)S(1)}, bf16[256,256]{1,0:T(8,128)(2,1)}, u32[]{:S(2)}) copy-start(bf16[256,256]{1,0:T(8,128)(2,1)} %w2s_ref.3) | copy-start | bytes 393220
  0.6 85.7 %copy-start.1 = (bf16[256,256]{1,0:T(8,128)(2,1)S(1)}, bf16[256,256]{1,0:T(8,128)(2,1)}, u32[]{:S(2)}) copy-start(bf16[256,256]{1,0:T(8,128)(2,1)} %w2n_ref.3) | copy-start | bytes 393220
  0.7 85.7 %copy-start.2 = (bf16[256,172]{0,1:T(8,128)(2,1)S(1)}, bf16[256,172]{0,1:T(8,128)(2,1)}, u32[]{:S(2)}) copy-start(bf16[256,172]{0,1:T(8,128)(2,1)} %param.21) | copy-start | bytes 264196
  0.7 85.7 %copy-start.3 = (s32[192]{0:T(256)S(1)}, s32[192]{0:T(256)}, u32[]{:S(2)}) copy-start(s32[192]{0:T(256)} %labels_ref.3) | copy-start | bytes 2308
  0.7 85.7 %copy-start.4 = (s32[192]{0:T(256)S(1)}, s32[192]{0:T(256)}, u32[]{:S(2)}) copy-start(s32[192]{0:T(256)} %counts_ref.1) | copy-start | bytes 2308
  71.5 14.8 %all-to-all-start.2 = ((bf16[12,24,256]{2,1,0:T(8,128)(2,1)}), bf16[12,24,256]{2,1,0:T(8,128)(2,1)S(1)}, u32[]{:S(2)}, u32[]{:S(2)}) async-start(bf16[12,24,256]{2,1,0:T(8,128)(2,1)} %bitcast.6), calls=%async_computation.2 | async-start | bytes 294912 | tf_op jit(solution)/shard_map/all_to_all | solution.py:395

commit v5 on v4

--- a/solution.py
+++ b/solution.py
@@ -39,7 +39,6 @@
 BF16 = jnp.bfloat16
 F32 = jnp.float32
 VMEM = pl.BlockSpec(memory_space=pltpu.VMEM)
-SMEM = pl.BlockSpec(memory_space=pltpu.SMEM)
 HBM = pl.BlockSpec(memory_space=pltpu.HBM)
 
 
@@ -270,8 +269,8 @@
     return jnp.sum(spread_out, axis=1, keepdims=True).astype(jnp.int32)
 
 
-def seeds_kernel(place_ref, z_ref, left_ref, counts_ref, labels_ref, w2s_ref, w2n_ref, w3_ref, o_ref, stage):
-    first = place_ref[0] * SEEDS_Y
+def seeds_kernel(z_ref, left_ref, counts_ref, labels_ref, w2s_ref, w2n_ref, w3_ref, o_ref, stage):
+    first = lax.axis_index("y") * SEEDS_Y
     counts = as_column(counts_ref, first, SEEDS_Y)
     scale = counts.astype(F32)
     pre_one = z_ref[...].astype(F32)[:ROWS_Y]
@@ -303,19 +302,19 @@
     o_ref[...] = stage[...].astype(BF16)
 
 
-def seeds(place, pre_one, left, counts, labels, w2_self, w2_nbr, w3):
+def seeds(pre_one, left, counts, labels, w2_self, w2_nbr, w3):
     return pl.pallas_call(
         seeds_kernel,
         out_shape=jax.ShapeDtypeStruct((Y * BACK, H), BF16),
-        in_specs=[SMEM] + [VMEM] * 7,
+        in_specs=[VMEM] * 7,
         out_specs=VMEM,
         scratch_shapes=[pltpu.VMEM((Y * BACK, H), F32)],
         compiler_params=pltpu.CompilerParams(vmem_limit_bytes=32 * 1024 * 1024),
         name="seeds",
-    )(place, pre_one, left, counts, labels, w2_self, w2_nbr, w3)
-
-
-def weights_kernel(r_ref, labels_ref, w2s_ref, w2n_ref, w3_ref, o_ref):
+    )(pre_one, left, counts, labels, w2_self, w2_nbr, w3)
+
+
+def weights_kernel(r_ref, labels_ref, w2s_ref, w2n_ref, w3_ref, keep_ref, send_ref, o_ref):
     rows = r_ref[...].astype(F32)
     grad_one = jnp.zeros((32, H), F32)
     head, mean_two = [], []
@@ -332,34 +331,38 @@
     o_ref[pl.ds(AT_THIRD, C), :] = inner_rows(grad_three, act_two)
     rest = 2 * HALF - AT_THIRD - C
     o_ref[pl.ds(AT_THIRD + C, rest), :] = jnp.zeros((rest, H), F32)
+    core = lax.axis_index("core")
+    keep_ref[...] = o_ref[pl.ds(pl.multiple_of(core * HALF, 8), HALF), :]
+    send_ref[...] = o_ref[pl.ds(pl.multiple_of((1 - core) * HALF, 8), HALF), :]
 
 
 def weights(received, labels, w2_self, w2_nbr, w3):
     return pl.pallas_call(
         weights_kernel,
-        out_shape=jax.ShapeDtypeStruct((2 * HALF, H), F32),
+        out_shape=(jax.ShapeDtypeStruct((HALF, H), F32), jax.ShapeDtypeStruct((HALF, H), F32)),
         in_specs=[VMEM] * 5,
-        out_specs=VMEM,
+        out_specs=(VMEM, VMEM),
+        scratch_shapes=[pltpu.VMEM((2 * HALF, H), F32)],
         compiler_params=pltpu.CompilerParams(vmem_limit_bytes=32 * 1024 * 1024),
         name="weights",
     )(received, labels, w2_self, w2_nbr, w3)
 
 
-def halve_kernel(g_ref, o_ref):
-    total = (g_ref[pl.ds(0, HALF), :] + g_ref[pl.ds(HALF, HALF), :]).astype(BF16)
+def halve_kernel(kept_ref, other_ref, o_ref):
+    total = (kept_ref[...] + other_ref[...]).astype(BF16)
     for x in range(X):
         o_ref[pl.ds(x * HALF, HALF), :] = total
 
 
-def halve(received):
+def halve(kept, other):
     return pl.pallas_call(
         halve_kernel,
         out_shape=jax.ShapeDtypeStruct((X * HALF, H), BF16),
-        in_specs=[VMEM],
+        in_specs=[VMEM, VMEM],
         out_specs=VMEM,
         compiler_params=pltpu.CompilerParams(vmem_limit_bytes=16 * 1024 * 1024),
         name="halve",
-    )(received)
+    )(kept, other)
 
 
 def finish_kernel(g_ref, w1s_ref, w1n_ref, w2s_ref, w2n_ref, w3_ref, sems):
@@ -400,10 +403,9 @@
     packed = gather(self_ids, nbr_ids.T, nbr_counts, features, w1_self, w1_nbr)
     shares, left = project(exchange(packed, "y", Y))
     pre_one = exchange(spread(exchange(shares, "z", Z)), "z", Z)
-    place = lax.axis_index("y").astype(jnp.int32)[None]
-    back = seeds(place, pre_one, left, seed_counts, labels, w2_self, w2_nbr, w3.T)
-    grads = weights(exchange(back, "y", Y), labels, w2_self, w2_nbr, w3.T)
-    grads = exchange(halve(exchange(grads, "core", CORE)), "x", X)
+    back = seeds(pre_one, left, seed_counts, labels, w2_self, w2_nbr, w3.T)
+    kept, sent = weights(exchange(back, "y", Y), labels, w2_self, w2_nbr, w3.T)
+    grads = exchange(halve(kept, lax.ppermute(sent, "core", [(0, 1), (1, 0)])), "x", X)
     summed = jnp.sum(grads.reshape(X, HALF, H).astype(F32), axis=0)
     whole = lax.all_gather(summed, "core", axis=0, tiled=True)
     grad_w1s, grad_w1n, grad_w2s, grad_w2n, grad_w3 = finish(whole)

time: 132 us -> 130 us (0.985)
  waiting for transfers between devices: 11.3 us -> 1.3 us
  blocking collectives: 85 us -> 89.9 us
  starting transfers between devices: 3.52 us -> 6.84 us
    all_to_all x1 -> x0, waiting for transfers between devices: 11.3 us -> none  [exchange(): lax.all_to_all(rows.reshape(parts, -1, rows.shape[1]), axis, 0, 0)]
    ppermute x0 -> x1, starting transfers between devices: none -> 6.84 us  [local(): lax.ppermute(sent, 'core', [(0, 1), (1, 0)])]
    all_to_all x5, blocking collectives: 81.3 us -> 86.2 us  [exchange(): lax.all_to_all(rows.reshape(parts, -1, rows.shape[1]), axis, 0, 0)]
    all_to_all x1 -> x0, starting transfers between devices: 3.52 us -> none  [exchange(): lax.all_to_all(rows.reshape(parts, -1, rows.shape[1]), axis, 0, 0)]
where the time goes in v5:
time: 130 us; the launch traced here: 129 us
  blocking collectives  89.9 us (69%)
  Pallas kernels  30.3 us (23%)
  starting transfers between devices  6.84 us (5%)
  waiting for transfers between devices  1.3 us (1%)
    all_to_all x5, blocking collectives, exchange(): lax.all_to_all(rows.reshape(parts, -1, rows.shape[1]), axis, 0, 0)  86.2 us
    pallas_call x1, Pallas kernels, gather(): pl.pallas_call(gather_kernel, out_shape=jax.ShapeDtypeStruct((Y * SEND, 1...  25.9 us
    ppermute x1, starting transfers between devices, local(): lax.ppermute(sent, 'core', [(0, 1), (1, 0)])  6.84 us
    all_gather x1, blocking collectives, local(): whole = lax.all_gather(summed, 'core', axis=0, tiled=True)  3.7 us
  transfers between devices with their start and end apart: 1, of which 1 were waited for; matrix products, arithmetic and copies ran while one was open for 0% of the time, Pallas kernels for 0%

profile of v5, /device:TPU:1, one launch (start us, length us, event | category | flops | bytes accessed | tf_op | source)
XLA Modules:
  0.0 129.2 jit_solution(11883721496988516196)
XLA Ops:
  0.6 0.0 copy-start
  0.6 0.0 copy-start.1
  0.7 0.0 copy-start.2
  0.7 0.0 copy-start.3
  0.7 0.0 copy-start.4
  0.7 25.9 %gather.1 = bf16[1152,128]{1,0:T(8,128)(2,1)} custom-call(s32[2112]{0:T(1024)} %self_in.1, s32[15,2112]{1,0:T(8,128)} %bitcast.23, s32[2112]{0:T(1024)} %counts_in.1, bf16[11,65536]{1,0:T(8,128)(2,1)} %x_in.1, bf16[11,256]{1,0:T(8,128)(2,1)} %w1s_in.1, bf16[11,256]{1,0:T(8,128)(2,1)} %w1n_in.1), custom_call_target="tpu_custom_call" | custom-call | tf_op jit(solution)/shard_map/gather/pallas_call | solution.py:154
  26.6 17.3 %all_to_all.25 = bf16[8,144,128]{2,1,0:T(8,128)(2,1)S(1)} all-to-all(bf16[8,144,128]{2,1,0:T(8,128)(2,1)} %bitcast.22), channel_id=1, replica_groups=mesh['z'=12,'y'=8,'x'=4,'core'=2] {'y'}, dimensions={0} | all-to-all | bytes 589824 | tf_op jit(solution)/shard_map/all_to_all | solution.py:398
  44.0 0.3 project.1
  44.3 26.6 %all_to_all.26 = bf16[12,24,256]{2,1,0:T(8,128)(2,1)S(1)} all-to-all(bf16[12,24,256]{2,1,0:T(8,128)(2,1)S(1)} %bitcast.21), channel_id=1, replica_groups=mesh['z'=12,'y'=8,'x'=4,'core'=2] {'z'}, dimensions={0} | all-to-all | bytes 294912 | tf_op jit(solution)/shard_map/all_to_all | solution.py:398
  70.9 13.4 %all_to_all.27 = bf16[12,24,256]{2,1,0:T(8,128)(2,1)S(1)} all-to-all(bf16[12,24,256]{2,1,0:T(8,128)(2,1)S(1)} %bitcast.17), channel_id=1, replica_groups=mesh['z'=12,'y'=8,'x'=4,'core'=2] {'z'}, dimensions={0} | all-to-all | bytes 294912 | tf_op jit(solution)/shard_map/all_to_all | solution.py:398
  84.3 0.0 copy-done
  84.3 0.0 copy-done.1
  84.3 0.0 copy-done.2
  84.3 0.0 copy-done.3
  84.3 1.5 %seeds.1 = bf16[640,256]{1,0:T(8,128)(2,1)S(1)} custom-call(bf16[288,256]{1,0:T(8,128)(2,1)S(1)} %bitcast.18, bf16[264,256]{1,0:T(8,128)(2,1)S(1)} %get-tuple-element.15.left_ref, s32[192]{0:T(256)S(1)} %copy-done.4, s32[192]{0:T(256)S(1)} %copy-done.3, bf16[256,256]{1,0:T(8,128)(2,1)S(1)} %copy-done, bf16[256,256]{1,0:T(8,128)(2,1)S(1)} %copy-done.1, ...), custom_call_target="tpu_custom_call" | custom-call | tf_op jit(solution)/shard_map/seeds/pallas_call | solution.py:306
  85.8 13.9 %all_to_all.28 = bf16[8,80,256]{2,1,0:T(8,128)(2,1)S(1)} all-to-all(bf16[8,80,256]{2,1,0:T(8,128)(2,1)S(1)} %bitcast.14), channel_id=1, replica_groups=mesh['z'=12,'y'=8,'x'=4,'core'=2] {'y'}, dimensions={0} | all-to-all | bytes 655360 | tf_op jit(solution)/shard_map/all_to_all | solution.py:398
  99.7 1.0 weights.1
  100.7 6.8 %collective-permute-start = (f32[368,256]{1,0:T(8,128)S(1)}, f32[368,256]{1,0:T(8,128)S(1)}, u32[]{:S(2)}, u32[]{:S(2)}) collective-permute-start(f32[368,256]{1,0:T(8,128)S(1)} %get-tuple-element.17), channel_id=1, source_target_pairs={{0,1},{1,0},{2,3},{3,2},{4,5},{5,4},{6,7},{7,6},{8,9},{9,8},{10,11... | collective-permute-start | bytes 1130504 | tf_op jit(solution)/shard_map/ppermute | solution.py:408
  107.6 1.3 %collective-permute-done.other_ref = f32[368,256]{1,0:T(8,128)S(1)} collective-permute-done((f32[368,256]{1,0:T(8,128)S(1)}, f32[368,256]{1,0:T(8,128)S(1)}, u32[]{:S(2)}, u32[]{:S(2)}) %collective-permute-start) | collective-permute-done | bytes 376864 | tf_op jit(solution)/shard_map/ppermute | solution.py:408
  108.9 0.1 halve.1
  108.9 15.0 %all_to_all.29 = bf16[4,368,256]{2,1,0:T(8,128)(2,1)S(1)} all-to-all(bf16[4,368,256]{2,1,0:T(8,128)(2,1)S(1)} %bitcast.12), channel_id=1, replica_groups=mesh['z'=12,'y'=8,'x'=4,'core'=2] {'x'}, dimensions={0} | all-to-all | bytes 1507328 | tf_op jit(solution)/shard_map/all_to_all | solution.py:398
  123.9 0.1 convert_reduce_fusion
  124.0 3.7 %all_gather.3.g_ref = f32[736,256]{1,0:T(8,128)S(1)} all-gather(f32[368,256]{1,0:T(8,128)S(1)} %convert_reduce_fusion), channel_id=1, replica_groups=mesh['z'=12,'y'=8,'x'=4,'core'=2] {'core'}, dimensions={0}, use_global_device_ids=true | all-gather | bytes 1130496 | tf_op jit(solution)/shard_map/all_gather | solution.py:410
  127.7 1.5 %finish.1 = (f32[11,256]{1,0:T(8,128)}, f32[11,256]{1,0:T(8,128)}, f32[256,256]{1,0:T(8,128)}, f32[256,256]{1,0:T(8,128)}, f32[172,256]{1,0:T(8,128)}) custom-call(f32[736,256]{1,0:T(8,128)S(1)} %all_gather.3.g_ref), custom_call_target="tpu_custom_call" | custom-call | tf_op jit(solution)/shard_map/finish/pallas_call | solution.py:386
  (2 shorter events, 0.0 us)
Async XLA Ops:
  0.6 83.7 %copy-start = (bf16[256,256]{1,0:T(8,128)(2,1)S(1)}, bf16[256,256]{1,0:T(8,128)(2,1)}, u32[]{:S(2)}) copy-start(bf16[256,256]{1,0:T(8,128)(2,1)} %w2s_ref.3) | copy-start | bytes 393220
  0.6 83.7 %copy-start.1 = (bf16[256,256]{1,0:T(8,128)(2,1)S(1)}, bf16[256,256]{1,0:T(8,128)(2,1)}, u32[]{:S(2)}) copy-start(bf16[256,256]{1,0:T(8,128)(2,1)} %w2n_ref.3) | copy-start | bytes 393220
  0.7 83.7 %copy-start.2 = (bf16[256,172]{0,1:T(8,128)(2,1)S(1)}, bf16[256,172]{0,1:T(8,128)(2,1)}, u32[]{:S(2)}) copy-start(bf16[256,172]{0,1:T(8,128)(2,1)} %param.21) | copy-start | bytes 264196
  0.7 83.7 %copy-start.3 = (s32[192]{0:T(256)S(1)}, s32[192]{0:T(256)}, u32[]{:S(2)}) copy-start(s32[192]{0:T(256)} %labels_ref.3) | copy-start | bytes 2308
  0.7 83.7 %copy-start.4 = (s32[192]{0:T(256)S(1)}, s32[192]{0:T(256)}, u32[]{:S(2)}) copy-start(s32[192]{0:T(256)} %counts_ref.1) | copy-start | bytes 2308
  100.7 8.2 %collective-permute-start = (f32[368,256]{1,0:T(8,128)S(1)}, f32[368,256]{1,0:T(8,128)S(1)}, u32[]{:S(2)}, u32[]{:S(2)}) collective-permute-start(f32[368,256]{1,0:T(8,128)S(1)} %get-tuple-element.17), channel_id=1, source_target_pairs={{0,1},{1,0},{2,3},{3,2},{4,5},{5,4},{6,7},{7,6},{8,9},{9,8},{10,11... | collective-permute-start | bytes 1130504 | tf_op jit(solution)/shard_map/ppermute | solution.py:408

commit v6 on v5

--- a/solution.py
+++ b/solution.py
@@ -31,9 +31,9 @@
 SEND = 144
 SHARE = 24
 ROWS_Z = Z * SHARE
-BACK = 32 + 2 * SEEDS_Y
+BACK = WIDE + 2 * SEEDS_Y
 AT_FIRST = 2 * H
-AT_THIRD = AT_FIRST + 32
+AT_THIRD = AT_FIRST + WIDE
 HALF = 368
 PIECES = 2
 BF16 = jnp.bfloat16
@@ -296,9 +296,11 @@
     grad = jnp.where(inner_rows(is_head, ones) > 0.5, outer_cols(grad_rows, w2s_ref[...]), grad)
     grad_one = inner_rows(left_ref[...], (grad * slope_one).astype(BF16))
     for y in range(Y):
-        stage[pl.ds(y * BACK, 32), :] = grad_one[y * 32 :][:32]
-        stage[pl.ds(y * BACK + 32, SEEDS_Y), :] = head.astype(F32)
-        stage[pl.ds(y * BACK + 32 + SEEDS_Y, SEEDS_Y), :] = mean_two.astype(F32)
+        both = grad_one[y * 32 :][:32]
+        none = jnp.zeros((WIDE - 2 * COLS, H), F32)
+        stage[pl.ds(y * BACK, WIDE), :] = jnp.concatenate([both[:COLS], both[16 : 16 + COLS], none], 0)
+        stage[pl.ds(y * BACK + WIDE, SEEDS_Y), :] = head.astype(F32)
+        stage[pl.ds(y * BACK + WIDE + SEEDS_Y, SEEDS_Y), :] = mean_two.astype(F32)
     o_ref[...] = stage[...].astype(BF16)
 
 
@@ -316,18 +318,18 @@
 
 def weights_kernel(r_ref, labels_ref, w2s_ref, w2n_ref, w3_ref, keep_ref, send_ref, o_ref):
     rows = r_ref[...].astype(F32)
-    grad_one = jnp.zeros((32, H), F32)
+    grad_one = jnp.zeros((WIDE, H), F32)
     head, mean_two = [], []
     for y in range(Y):
-        grad_one = grad_one + rows[y * BACK :][:32]
-        head.append(rows[y * BACK + 32 :][:SEEDS_Y])
-        mean_two.append(rows[y * BACK + 32 + SEEDS_Y :][:SEEDS_Y])
+        grad_one = grad_one + rows[y * BACK :][:WIDE]
+        head.append(rows[y * BACK + WIDE :][:SEEDS_Y])
+        mean_two.append(rows[y * BACK + WIDE + SEEDS_Y :][:SEEDS_Y])
     head = jnp.concatenate(head, 0).astype(BF16)
     mean_two = jnp.concatenate(mean_two, 0).astype(BF16)
     act_two, grad_three, grad_two = top(head, mean_two, as_column(labels_ref, 0, SEEDS_B), w2s_ref[...], w2n_ref[...], w3_ref[...])
     o_ref[pl.ds(0, H), :] = inner_rows(head, grad_two)
     o_ref[pl.ds(H, H), :] = inner_rows(mean_two, grad_two)
-    o_ref[pl.ds(AT_FIRST, 32), :] = grad_one
+    o_ref[pl.ds(AT_FIRST, WIDE), :] = grad_one
     o_ref[pl.ds(AT_THIRD, C), :] = inner_rows(grad_three, act_two)
     rest = 2 * HALF - AT_THIRD - C
     o_ref[pl.ds(AT_THIRD + C, rest), :] = jnp.zeros((rest, H), F32)
@@ -372,9 +374,9 @@
     ]
     for copy in copies:
         copy.start()
-    first = g_ref[pl.ds(AT_FIRST, 32), :]
+    first = g_ref[pl.ds(AT_FIRST, WIDE), :]
     w1s_ref[...] = first[:COLS]
-    w1n_ref[...] = first[16 : 16 + COLS]
+    w1n_ref[...] = first[COLS : 2 * COLS]
     w3_ref[...] = g_ref[pl.ds(AT_THIRD, C), :]
     for copy in copies:
         copy.wait()

time: 130 us -> 129 us (level)
  no operation moved by 1% of the time
where the time goes in v6:
time: 129 us
  blocking collectives  89.4 us (69%)
  Pallas kernels  30.3 us (23%)
  starting transfers between devices  6.94 us (5%)
  waiting for transfers between devices  1.3 us (1%)
    all_to_all x5, blocking collectives, exchange(): lax.all_to_all(rows.reshape(parts, -1, rows.shape[1]), axis, 0, 0)  85.7 us
    pallas_call x1, Pallas kernels, gather(): pl.pallas_call(gather_kernel, out_shape=jax.ShapeDtypeStruct((Y * SEND, 1...  25.9 us
    ppermute x1, starting transfers between devices, local(): lax.ppermute(sent, 'core', [(0, 1), (1, 0)])  6.94 us
    all_gather x1, blocking collectives, local(): whole = lax.all_gather(summed, 'core', axis=0, tiled=True)  3.7 us
  transfers between devices with their start and end apart: 1, of which 1 were waited for; matrix products, arithmetic and copies ran while one was open for 0% of the time, Pallas kernels for 0%

profile of v6, /device:TPU:1, one launch (start us, length us, event | category | flops | bytes accessed | tf_op | source)
XLA Modules:
  0.0 128.8 jit_solution(4255802621522480520)
XLA Ops:
  0.6 0.0 copy-start
  0.6 0.0 copy-start.1
  0.7 0.0 copy-start.2
  0.7 0.0 copy-start.3
  0.7 0.0 copy-start.4
  0.7 25.9 %gather.1 = bf16[1152,128]{1,0:T(8,128)(2,1)} custom-call(s32[2112]{0:T(1024)} %self_in.1, s32[15,2112]{1,0:T(8,128)} %bitcast.23, s32[2112]{0:T(1024)} %counts_in.1, bf16[11,65536]{1,0:T(8,128)(2,1)} %x_in.1, bf16[11,256]{1,0:T(8,128)(2,1)} %w1s_in.1, bf16[11,256]{1,0:T(8,128)(2,1)} %w1n_in.1), custom_call_target="tpu_custom_call" | custom-call | tf_op jit(solution)/shard_map/gather/pallas_call | solution.py:154
  26.6 17.3 %all_to_all.25 = bf16[8,144,128]{2,1,0:T(8,128)(2,1)S(1)} all-to-all(bf16[8,144,128]{2,1,0:T(8,128)(2,1)} %bitcast.22), channel_id=1, replica_groups=mesh['z'=12,'y'=8,'x'=4,'core'=2] {'y'}, dimensions={0} | all-to-all | bytes 589824 | tf_op jit(solution)/shard_map/all_to_all | solution.py:400
  44.0 0.3 project.1
  44.3 26.6 %all_to_all.26 = bf16[12,24,256]{2,1,0:T(8,128)(2,1)S(1)} all-to-all(bf16[12,24,256]{2,1,0:T(8,128)(2,1)S(1)} %bitcast.21), channel_id=1, replica_groups=mesh['z'=12,'y'=8,'x'=4,'core'=2] {'z'}, dimensions={0} | all-to-all | bytes 294912 | tf_op jit(solution)/shard_map/all_to_all | solution.py:400
  70.9 13.4 %all_to_all.27 = bf16[12,24,256]{2,1,0:T(8,128)(2,1)S(1)} all-to-all(bf16[12,24,256]{2,1,0:T(8,128)(2,1)S(1)} %bitcast.18), channel_id=1, replica_groups=mesh['z'=12,'y'=8,'x'=4,'core'=2] {'z'}, dimensions={0} | all-to-all | bytes 294912 | tf_op jit(solution)/shard_map/all_to_all | solution.py:400
  84.3 0.0 copy-done
  84.3 0.0 copy-done.1
  84.3 0.0 copy-done.2
  84.3 0.0 copy-done.3
  84.3 1.5 %seeds.1 = bf16[576,256]{1,0:T(8,128)(2,1)S(1)} custom-call(bf16[288,256]{1,0:T(8,128)(2,1)S(1)} %bitcast.16, bf16[264,256]{1,0:T(8,128)(2,1)S(1)} %get-tuple-element.15.left_ref, s32[192]{0:T(256)S(1)} %copy-done.4, s32[192]{0:T(256)S(1)} %copy-done.3, bf16[256,256]{1,0:T(8,128)(2,1)S(1)} %copy-done, bf16[256,256]{1,0:T(8,128)(2,1)S(1)} %copy-done.1, ...), custom_call_target="tpu_custom_call" | custom-call | tf_op jit(solution)/shard_map/seeds/pallas_call | solution.py:308
  85.9 13.4 %all_to_all.28 = bf16[8,72,256]{2,1,0:T(8,128)(2,1)S(1)} all-to-all(bf16[8,72,256]{2,1,0:T(8,128)(2,1)S(1)} %bitcast.14), channel_id=1, replica_groups=mesh['z'=12,'y'=8,'x'=4,'core'=2] {'y'}, dimensions={0} | all-to-all | bytes 589824 | tf_op jit(solution)/shard_map/all_to_all | solution.py:400
  99.3 1.0 weights.1
  100.3 6.9 %collective-permute-start = (f32[368,256]{1,0:T(8,128)S(1)}, f32[368,256]{1,0:T(8,128)S(1)}, u32[]{:S(2)}, u32[]{:S(2)}) collective-permute-start(f32[368,256]{1,0:T(8,128)S(1)} %get-tuple-element.17), channel_id=1, source_target_pairs={{0,1},{1,0},{2,3},{3,2},{4,5},{5,4},{6,7},{7,6},{8,9},{9,8},{10,11... | collective-permute-start | bytes 1130504 | tf_op jit(solution)/shard_map/ppermute | solution.py:410
  107.2 1.3 %collective-permute-done.other_ref = f32[368,256]{1,0:T(8,128)S(1)} collective-permute-done((f32[368,256]{1,0:T(8,128)S(1)}, f32[368,256]{1,0:T(8,128)S(1)}, u32[]{:S(2)}, u32[]{:S(2)}) %collective-permute-start) | collective-permute-done | bytes 376864 | tf_op jit(solution)/shard_map/ppermute | solution.py:410
  108.5 0.1 halve.1
  108.6 15.0 %all_to_all.29 = bf16[4,368,256]{2,1,0:T(8,128)(2,1)S(1)} all-to-all(bf16[4,368,256]{2,1,0:T(8,128)(2,1)S(1)} %bitcast.12), channel_id=1, replica_groups=mesh['z'=12,'y'=8,'x'=4,'core'=2] {'x'}, dimensions={0} | all-to-all | bytes 1507328 | tf_op jit(solution)/shard_map/all_to_all | solution.py:400
  123.6 0.1 convert_reduce_fusion
  123.7 3.7 %all_gather.3.g_ref = f32[736,256]{1,0:T(8,128)S(1)} all-gather(f32[368,256]{1,0:T(8,128)S(1)} %convert_reduce_fusion), channel_id=1, replica_groups=mesh['z'=12,'y'=8,'x'=4,'core'=2] {'core'}, dimensions={0}, use_global_device_ids=true | all-gather | bytes 1130496 | tf_op jit(solution)/shard_map/all_gather | solution.py:412
  127.4 1.5 %finish.1 = (f32[11,256]{1,0:T(8,128)}, f32[11,256]{1,0:T(8,128)}, f32[256,256]{1,0:T(8,128)}, f32[256,256]{1,0:T(8,128)}, f32[172,256]{1,0:T(8,128)}) custom-call(f32[736,256]{1,0:T(8,128)S(1)} %all_gather.3.g_ref), custom_call_target="tpu_custom_call" | custom-call | tf_op jit(solution)/shard_map/finish/pallas_call | solution.py:388
  (2 shorter events, 0.0 us)
Async XLA Ops:
  0.6 83.7 %copy-start = (bf16[256,256]{1,0:T(8,128)(2,1)S(1)}, bf16[256,256]{1,0:T(8,128)(2,1)}, u32[]{:S(2)}) copy-start(bf16[256,256]{1,0:T(8,128)(2,1)} %w2s_ref.3) | copy-start | bytes 393220
  0.6 83.7 %copy-start.1 = (bf16[256,256]{1,0:T(8,128)(2,1)S(1)}, bf16[256,256]{1,0:T(8,128)(2,1)}, u32[]{:S(2)}) copy-start(bf16[256,256]{1,0:T(8,128)(2,1)} %w2n_ref.3) | copy-start | bytes 393220
  0.7 83.7 %copy-start.2 = (bf16[256,172]{0,1:T(8,128)(2,1)S(1)}, bf16[256,172]{0,1:T(8,128)(2,1)}, u32[]{:S(2)}) copy-start(bf16[256,172]{0,1:T(8,128)(2,1)} %param.21) | copy-start | bytes 264196
  0.7 83.7 %copy-start.3 = (s32[192]{0:T(256)S(1)}, s32[192]{0:T(256)}, u32[]{:S(2)}) copy-start(s32[192]{0:T(256)} %labels_ref.3) | copy-start | bytes 2308
  0.7 83.7 %copy-start.4 = (s32[192]{0:T(256)S(1)}, s32[192]{0:T(256)}, u32[]{:S(2)}) copy-start(s32[192]{0:T(256)} %counts_ref.1) | copy-start | bytes 2308
  100.3 8.3 %collective-permute-start = (f32[368,256]{1,0:T(8,128)S(1)}, f32[368,256]{1,0:T(8,128)S(1)}, u32[]{:S(2)}, u32[]{:S(2)}) collective-permute-start(f32[368,256]{1,0:T(8,128)S(1)} %get-tuple-element.17), channel_id=1, source_target_pairs={{0,1},{1,0},{2,3},{3,2},{4,5},{5,4},{6,7},{7,6},{8,9},{9,8},{10,11... | collective-permute-start | bytes 1130504 | tf_op jit(solution)/shard_map/ppermute | solution.py:410
